TPU v7x, 512 devices: a whole 4x8x8 slice. The times are simulated.
512 devices in a mesh: st: 128 (over z, x, y_lo), tb: 4 (over y_hi, core).
Axes of the slice: x: 4, y: 8 (y_hi: 2, y_lo: 4; y = y_hi * 4 + y_lo), z: 8, core: 2. Of those that a mesh axis runs over, the one named last changes fastest.
Arguments:
- voltages: bfloat16 [1024, 98304], P('st', 'tb'), may hold values from -6 to 6
- fir_taps: float32 [12, 512], replicated, may hold values from -1.75 to 1.75
Outputs:
- visibilities: float32 [2, 128, 1024, 1024], P(None, 'st', 'tb')
All inputs are finite; a program needn't handle non-finite values.
Results may differ from a plain program's by a relative error of at most 0.0037.
Values may be sent and summed in bfloat16 or wider, within the bound.
No kernel may reach another device: no remote copies, remote signals or barrier semaphores. Data moves between devices by JAX's collectives and lax.ppermute only.
A program may use at most 64 MiB of HBM per device.

v0:
```python
import math

import jax
import jax.numpy as jnp
from jax import lax
from jax.sharding import PartitionSpec as P

CH = 128
OFFSET = 64


def passed_along(array, axis, by):
    devices = lax.axis_size(axis)
    pairs = [(i, i + by) for i in range(devices) if 0 <= i + by < devices]
    return lax.ppermute(array, axis, pairs)


def apply_taps(extended, fir_taps, count):
    taps = fir_taps.shape[0]
    filtered = jnp.zeros((extended.shape[0], count, extended.shape[2]), jnp.float32)
    for tap in range(taps):
        filtered = filtered + fir_taps[tap] * extended[:, tap : tap + count, :]
    return filtered


def correlate(own_rows, columns):
    n_ch, n_cols, length = columns.shape
    pairs = columns.reshape(n_ch, n_cols, length // 2, 2)
    rotated = jnp.stack([-pairs[:, :, :, 1], pairs[:, :, :, 0]], 3).reshape(n_ch, n_cols, length)
    real_vis = jnp.einsum("crl,cjl->crj", own_rows, columns, preferred_element_type=jnp.float32)
    imag_vis = jnp.einsum("crl,cjl->crj", own_rows, rotated, preferred_element_type=jnp.float32)
    return jnp.stack([real_vis, imag_vis], 0)


def per_device(voltages, fir_taps):
    in_dev, length = voltages.shape
    taps, frame = fir_taps.shape
    frames_dev = length // frame
    margin = taps - 1
    blocks = voltages.reshape(in_dev, frames_dev, frame)
    earlier = passed_along(blocks[:, frames_dev - margin :, :], "tb", 1)
    extended = jnp.concatenate([earlier, blocks], 1)
    filtered = apply_taps(extended, fir_taps, frames_dev)
    sample_idx = jnp.arange(frame, dtype=jnp.int32)[None, :]
    channel_idx = jnp.arange(CH, dtype=jnp.int32)[:, None] + OFFSET
    phase = sample_idx * channel_idx % frame
    angle = phase.astype(jnp.float32) * (2.0 * math.pi / frame)
    table = jnp.stack([jnp.cos(angle), -jnp.sin(angle)], 0) / math.sqrt(frame)
    spectra = jnp.einsum(
        "pcn,ifn->cifp",
        table,
        filtered,
        precision=lax.Precision.HIGHEST,
        preferred_element_type=jnp.float32,
    )
    spectra = spectra.astype(jnp.bfloat16).reshape(CH, in_dev, frames_dev * 2)
    n_blocks = lax.axis_size("tb")
    n_inputs = in_dev * lax.axis_size("st")
    rows = n_inputs // n_blocks
    row_start = lax.axis_index("tb") * rows
    window = lax.all_gather(spectra, "tb", axis=2, tiled=True)
    turned = lax.all_to_all(window, "st", split_axis=0, concat_axis=1, tiled=True)
    own_rows = lax.dynamic_slice_in_dim(turned, row_start, rows, 1)
    summed = correlate(own_rows, turned)
    return summed / jnp.float32(frames_dev * n_blocks)


def solution(mesh):
    in_specs = (P("st", "tb"), P())
    out_specs = P(None, "st", "tb", None)
    return jax.shard_map(
        per_device, mesh=mesh, in_specs=in_specs, out_specs=out_specs, check_vma=False
    )
```

profile of v0, /device:TPU:1, one launch (start us, length us, event | category | flops | bytes accessed | tf_op | source)
XLA Modules:
  0.0 113.4 jit_solution(7077188448487761612)
XLA Ops:
  0.0 1.1 copy.26
  1.2 8.8 %collective-permute-start = (bf16[8,11,512]{2,1,0:T(8,128)(2,1)S(1)}, bf16[8,11,512]{2,1,0:T(8,128)(2,1)S(1)}, u32[]{:S(2)}, u32[]{:S(2)}) collective-permute-start(bf16[8,11,512]{2,1,0:T(8,128)(2,1)S(1)} %slice.104), channel_id=1, source_target_pairs={{0,1},{1,2},{2,3},{4,5},{5,6},{6,7},{8,9},{9,10},{10,11},{12,13},{... | collective-permute-start | bytes 270344 | tf_op jit(solution)/shard_map/ppermute | solution.py:15
  10.0 1.1 fusion.86
  11.1 1.0 fusion.92
  12.2 0.0 collective-permute-done
  12.2 2.1 %fusion = bf16[128,8,48,2]{0,2,3,1:T(8,128)(2,1)S(1)} fusion(bf16[8,48,512]{2,1,0:T(8,128)(2,1)S(1)} %copy.26, f32[1,128,512]{2,1,0:T(8,128)S(1)} %get-tuple-element.20, f32[1,128,512]{2,1,0:T(8,128)S(1)} %get-tuple-element.19, bf16[8,11,512]{2,1,0:T(8,128)(2,1)S(1)} %collective-permute-done, f32[512]{0:T(512)S(1)} %bitcast.56, f32[512]{0:T(512)S(1)} %bitcast.57, ...), kind=kOutput, calls=%fused_computation.14 | convolution fusion | flops 617709568 | bytes 1228800 | tf_op jit(solution)/shard_map/pcn,ifn->cifp/dot_general | solution.py:49
  14.3 0.1 copy.29
  14.3 15.7 %all_gather.3 = bf16[128,8,384]{0,1,2:T(8,128)(2,1)S(1)} all-gather(bf16[128,8,96]{0,1,2:T(8,128)(2,1)S(1)} %bitcast.44), channel_id=1, replica_groups=mesh['st'=128,'tb'=4] {'tb'}, dimensions={2}, use_global_device_ids=true | all-gather | bytes 983040 | tf_op jit(solution)/shard_map/all_gather | solution.py:61
  30.0 1.6 %copy.30 = bf16[128,8,384]{2,1,0:T(8,128)(2,1)} copy(bf16[128,8,384]{0,1,2:T(8,128)(2,1)S(1)} %all_gather.3) | data formatting | bytes 1572864 | tf_op jit(solution)/shard_map/all_gather | solution.py:61
  31.6 17.4 %all-to-all-start = ((bf16[128,8,384]{2,1,0:T(8,128)(2,1)}), bf16[128,8,384]{2,1,0:T(8,128)(2,1)S(1)}, u32[]{:S(2)}, u32[]{:S(2)}) async-start(bf16[128,8,384]{2,1,0:T(8,128)(2,1)} %copy.30), calls=%async_computation | async-start | bytes 1572864 | tf_op jit(solution)/shard_map/all_to_all | solution.py:62
  49.0 24.7 %all-to-all-done = bf16[128,8,384]{2,1,0:T(8,128)(2,1)S(1)} async-done(((bf16[128,8,384]{2,1,0:T(8,128)(2,1)}), bf16[128,8,384]{2,1,0:T(8,128)(2,1)S(1)}, u32[]{:S(2)}, u32[]{:S(2)}) %all-to-all-start) | async-done | bytes 786464 | tf_op jit(solution)/shard_map/all_to_all | solution.py:62
  73.8 17.1 %copy.31 = bf16[128,8,384]{1,0,2:T(8,128)(2,1)} copy(bf16[128,8,384]{2,1,0:T(8,128)(2,1)S(1)} %all-to-all-done) | data formatting | bytes 1572864 | tf_op jit(solution)/shard_map/all_to_all | solution.py:62
  90.9 16.2 %reshape.190 = bf16[1,1024,192,2]{1,3,2,0:T(2,128)(2,1)S(1)} reshape(bf16[128,8,384]{1,0,2:T(8,128)(2,1)} %copy.31) | data formatting | bytes 1572864 | tf_op jit(solution)/shard_map/reshape | solution.py:28
  107.1 1.7 %slice_negate_fusion = (bf16[1,1024,192,1]{1,3,2,0:T(2,128)(2,1)S(1)}, bf16[1,1024,192,1]{1,3,2,0:T(2,128)(2,1)S(1)}) fusion(bf16[1,1024,192,2]{1,3,2,0:T(2,128)(2,1)S(1)} %reshape.190), kind=kLoop, calls=%fused_computation.15 | loop fusion | flops 196608 | bytes 1572864 | tf_op jit(solution)/shard_map/neg | solution.py:29
  108.8 1.8 %pad_maximum_fusion = bf16[1,1024,192,2]{1,3,2,0:T(2,128)(2,1)S(1)} fusion(bf16[1,1024,192,1]{1,3,2,0:T(2,128)(2,1)S(1)} %get-tuple-element.6, bf16[1,1024,192,1]{1,3,2,0:T(2,128)(2,1)S(1)} %get-tuple-element.5), kind=kLoop, calls=%fused_computation.16 | loop fusion | flops 1572864 | bytes 1572864 | tf_op jit(solution)/shard_map/stack | solution.py:29
  110.6 0.3 reshape.191
  110.9 0.4 convolution_bitcast_fusion
  111.4 0.5 convolution_bitcast_fusion.1
  111.9 1.5 %maximum_multiply_fusion = f32[2,1,256,1024]{3,2,1,0:T(8,128)} fusion(f32[1,1,256,1024]{3,2,1,0:T(8,128)S(1)} %convolution_bitcast_fusion, f32[1,1,256,1024]{3,2,1,0:T(8,128)S(1)} %convolution_bitcast_fusion.1), kind=kLoop, calls=%fused_computation | loop fusion | flops 1048576 | bytes 4194304 | tf_op jit(solution)/shard_map/div | solution.py:65
  (2 shorter events, 0.0 us)
Async XLA Ops:
  1.2 11.0 %collective-permute-start = (bf16[8,11,512]{2,1,0:T(8,128)(2,1)S(1)}, bf16[8,11,512]{2,1,0:T(8,128)(2,1)S(1)}, u32[]{:S(2)}, u32[]{:S(2)}) collective-permute-start(bf16[8,11,512]{2,1,0:T(8,128)(2,1)S(1)} %slice.104), channel_id=1, source_target_pairs={{0,1},{1,2},{2,3},{4,5},{5,6},{6,7},{8,9},{9,10},{10,11},{12,13},{... | collective-permute-start | bytes 270344 | tf_op jit(solution)/shard_map/ppermute | solution.py:15
  31.6 42.1 %all-to-all-start = ((bf16[128,8,384]{2,1,0:T(8,128)(2,1)}), bf16[128,8,384]{2,1,0:T(8,128)(2,1)S(1)}, u32[]{:S(2)}, u32[]{:S(2)}) async-start(bf16[128,8,384]{2,1,0:T(8,128)(2,1)} %copy.30), calls=%async_computation | async-start | bytes 1572864 | tf_op jit(solution)/shard_map/all_to_all | solution.py:62
where the time goes:
time: 114 us; the launch traced here: 113 us
  local copies, waits for them, and re-layouts  37.5 us (33%)
  starting transfers between devices  26.2 us (23%)
  waiting for transfers between devices  24.7 us (22%)
  blocking collectives  15.7 us (14%)
  other arithmetic  6.15 us (5%)
  matrix products  2.97 us (3%)
    all_to_all x1, waiting for transfers between devices, per_device(): lax.all_to_all(window, 'st', split_axis=0, concat_axis=1, tiled=True)  24.7 us
    all_to_all x1, starting transfers between devices, per_device(): lax.all_to_all(window, 'st', split_axis=0, concat_axis=1, tiled=True)  17.4 us
    all_to_all x1, local copies, waits for them, and re-layouts, per_device(): lax.all_to_all(window, 'st', split_axis=0, concat_axis=1, tiled=True)  17.1 us
    reshape x1, local copies, waits for them, and re-layouts, correlate(): pairs = columns.reshape(n_ch, n_cols, length // 2, 2)  16.2 us
    all_gather x1, blocking collectives, per_device(): window = lax.all_gather(spectra, 'tb', axis=2, tiled=True)  15.7 us
    ppermute x1, starting transfers between devices, passed_along(): return lax.ppermute(array, axis, pairs)  8.84 us
  transfers between devices with their start and end apart: 2, of which 1 were waited for; matrix products, arithmetic and copies ran while one was open for 2% of the time, Pallas kernels for 0%

commit v1 on v0

v1 whole, which is shorter than its diff:
```python
import math

import jax
import jax.numpy as jnp
import numpy as np
from jax import lax
from jax.experimental import pallas as pl
from jax.experimental.pallas import tpu as pltpu
from jax.sharding import Mesh
from jax.sharding import PartitionSpec as P

CH = 128
OFFSET = 64
FRAME = 512
TAPS = 12
N_IN = 8
N_FR = 48
N_TB = 4
N_ZX = 32
N_Y = 4
PIECE = 2 * N_FR
WIDTH = N_Y * PIECE
LANES = 128
VMEM = pl.BlockSpec(memory_space=pltpu.VMEM)
PARAMS = pltpu.CompilerParams(vmem_limit_bytes=40 * 1024 * 1024)


def dft_tables():
    ylo = np.arange(N_Y)[:, None, None]
    part = np.arange(2)[None, :, None]
    zx = np.arange(N_ZX)[None, None, :]
    channel = (zx * N_Y + ylo + 0 * part).reshape(-1) + OFFSET
    is_im = (part + 0 * ylo + 0 * zx).reshape(-1)
    phase = channel[:, None] * np.arange(FRAME)[None, :] % FRAME
    angle = phase * (2.0 * math.pi / FRAME)
    table = np.where(is_im[:, None] == 1, -np.sin(angle), np.cos(angle)) / math.sqrt(FRAME)
    high = table.astype(jnp.bfloat16)
    low = (table - high.astype(np.float64)).astype(jnp.bfloat16)
    return high, low


def lane_ids(rows):
    return lax.broadcasted_iota(jnp.int32, (rows, LANES), 1)


def turned(block, shift):
    shift %= LANES
    return block if shift == 0 else pltpu.roll(block, shift, 1)


def dot_t(a, b):
    return lax.dot_general(a, b, (((1,), (1,)), ((), ())), preferred_element_type=jnp.float32)


def channelize_kernel(halo_ref, volt_ref, taps_ref, high_ref, low_ref, out_ref, filt, fhigh, flow, spread):
    margin = TAPS - 1
    for block in range(FRAME // LANES):
        lo = block * LANES
        taps = [jnp.broadcast_to(taps_ref[k : k + 1, lo : lo + LANES], (N_IN, LANES)) for k in range(TAPS)]
        window = []
        for t in range(N_FR + margin):
            if t < margin:
                v = halo_ref[:, t * FRAME + lo : t * FRAME + lo + LANES]
            else:
                v = volt_ref[:, (t - margin) * FRAME + lo : (t - margin) * FRAME + lo + LANES]
            window.append(v.astype(jnp.float32))
            if t < margin:
                continue
            total = taps[0] * window[0]
            for k in range(1, TAPS):
                total = total + taps[k] * window[k]
            window.pop(0)
            f = t - margin
            filt[block, f * N_IN : (f + 1) * N_IN, :] = total
    for i in range(N_IN):
        for block in range(FRAME // LANES):
            lo = block * LANES
            x = filt[block, pl.ds(i, N_FR, stride=N_IN), :]
            high = x.astype(jnp.bfloat16)
            low = (x - high.astype(jnp.float32)).astype(jnp.bfloat16)
            fhigh[i * 64 : i * 64 + N_FR, lo : lo + LANES] = high
            flow[i * 64 : i * 64 + N_FR, lo : lo + LANES] = low
        zero = jnp.zeros((64 - N_FR, FRAME), jnp.bfloat16)
        fhigh[i * 64 + N_FR : (i + 1) * 64, :] = zero
        flow[i * 64 + N_FR : (i + 1) * 64, :] = zero
    lanes = lane_ids(N_ZX)
    for pair in range(N_IN // 2):
        fh = fhigh[pair * LANES : (pair + 1) * LANES, :]
        fl = flow[pair * LANES : (pair + 1) * LANES, :]
        spec = dot_t(high_ref[...], fh) + (dot_t(high_ref[...], fl) + dot_t(low_ref[...], fh))
        for sub in range(2):
            i = pair * 2 + sub
            tiles = [jnp.zeros((N_ZX, LANES), jnp.float32) for _ in range(WIDTH // LANES)]
            for j in range(2 * N_Y):
                rows = spec[j * N_ZX : (j + 1) * N_ZX, :]
                start = j * N_FR
                rolled = turned(rows, start - sub * 64)
                for t in range(start // LANES, (start + N_FR - 1) // LANES + 1):
                    first = max(start - t * LANES, 0)
                    last = min(start + N_FR - t * LANES, LANES)
                    tiles[t] = jnp.where((lanes >= first) & (lanes < last), rolled, tiles[t])
            for t in range(WIDTH // LANES):
                spread[t, pl.ds(i, N_ZX, stride=N_IN), :] = tiles[t]
    for t in range(WIDTH // LANES):
        out_ref[:, t * LANES : (t + 1) * LANES] = spread[t].astype(jnp.bfloat16)


def move_lanes(sources, start, width, to, tiles, lanes):
    done = 0
    while done < width:
        src, dst = start + done, to + done
        n = min(width - done, LANES - src % LANES, LANES - dst % LANES)
        t = dst // LANES
        rolled = turned(sources[src // LANES], dst - src)
        first = dst % LANES
        if n == LANES:
            tiles[t] = rolled
        else:
            tiles[t] = jnp.where((lanes >= first) & (lanes < first + n), rolled, tiles[t])
        done += n


def repack_kernel(in_ref, out_ref):
    rows = 64
    lanes = lane_ids(rows)
    n_tiles = WIDTH // LANES
    zero = jnp.zeros((rows, LANES), jnp.float32)
    data = in_ref[...].astype(jnp.float32).reshape(8, 4, N_IN, WIDTH)
    parts = []
    for q in range(4):
        x = data[:, q].reshape(rows, WIDTH)
        parts.append([x[:, t * LANES : (t + 1) * LANES] for t in range(n_tiles)])
    for k in range(N_Y):
        tiles = [zero] * n_tiles
        for q in range(4):
            move_lanes(parts[q], k * PIECE, PIECE, q * PIECE, tiles, lanes)
        for t in range(n_tiles):
            value = tiles[t].astype(jnp.bfloat16)
            out_ref[k * rows : (k + 1) * rows, t * LANES : (t + 1) * LANES] = value
            out_ref[(N_Y + k) * rows : (N_Y + k + 1) * rows, t * LANES : (t + 1) * LANES] = value


def unpack_kernel(in_ref, out_ref):
    rows = 64
    lanes = lane_ids(rows)
    n_tiles = WIDTH // LANES
    zero = jnp.zeros((rows, LANES), jnp.float32)
    for q in range(4):
        for p in range(2):
            cols = []
            for k in range(N_Y):
                tiles = [zero]
                for h in range(2):
                    base = (h * N_Y + k) * rows
                    start = q * PIECE + p * N_FR
                    need = range(start // LANES, (start + N_FR - 1) // LANES + 1)
                    src = {
                        t: in_ref[base : base + rows, t * LANES : (t + 1) * LANES].astype(jnp.float32)
                        for t in need
                    }
                    move_lanes(src, start, N_FR, h * N_FR, tiles, lanes)
                cols.append(tiles[0].reshape(8, N_IN, LANES))
            value = jnp.concatenate(cols, axis=1)
            out_ref[:, q, :, p * LANES : (p + 1) * LANES] = value.astype(jnp.bfloat16)


def correlate_kernel(scale, row_ref, all_ref, out_ref):
    rows = out_ref.shape[2]
    cols = out_ref.shape[3]
    own = pl.multiple_of(row_ref[0], rows)
    col = pl.multiple_of(pl.program_id(0) * cols, cols)
    a0 = all_ref[0, pl.ds(own, rows), :]
    a1 = all_ref[1, pl.ds(own, rows), :]
    b = jnp.concatenate([all_ref[0, pl.ds(col, cols), :], all_ref[1, pl.ds(col, cols), :]], axis=1)
    plain = jnp.concatenate([a0, a1], axis=1)
    crossed = jnp.concatenate([a0[:, LANES:], -a0[:, :LANES], a1[:, LANES:], -a1[:, :LANES]], axis=1)
    out_ref[0, 0] = dot_t(plain, b) * scale
    out_ref[1, 0] = dot_t(crossed, b) * scale


def per_device(voltages, fir_taps):
    in_dev, length = voltages.shape
    margin = (TAPS - 1) * FRAME
    tail = voltages[:, length - margin :]
    halo = lax.ppermute(tail, ("yhi", "core"), [(i, i + 1) for i in range(N_TB - 1)])
    high, low = dft_tables()
    spectra = pl.pallas_call(
        channelize_kernel,
        out_shape=jax.ShapeDtypeStruct((N_ZX * N_IN, WIDTH), jnp.bfloat16),
        in_specs=[VMEM] * 5,
        out_specs=VMEM,
        scratch_shapes=[
            pltpu.VMEM((FRAME // LANES, N_FR * N_IN, LANES), jnp.float32),
            pltpu.VMEM((64 * N_IN, FRAME), jnp.bfloat16),
            pltpu.VMEM((64 * N_IN, FRAME), jnp.bfloat16),
            pltpu.VMEM((WIDTH // LANES, N_ZX * N_IN, LANES), jnp.float32),
        ],
        compiler_params=PARAMS,
        name="channelize",
    )(halo, voltages, fir_taps, jnp.asarray(high), jnp.asarray(low))
    first = lax.all_to_all(spectra.reshape(N_ZX, N_IN, WIDTH), ("z", "x"), 0, 0, tiled=True)
    packed = pl.pallas_call(
        repack_kernel,
        out_shape=jax.ShapeDtypeStruct((2 * N_Y * 64, WIDTH), jnp.bfloat16),
        in_specs=[VMEM],
        out_specs=VMEM,
        compiler_params=PARAMS,
        name="repack",
    )(first.reshape(N_ZX * N_IN, WIDTH))
    second = lax.all_to_all(packed.reshape(2 * N_Y, 64, WIDTH), ("yhi", "ylo"), 0, 0, tiled=True)
    half = pl.pallas_call(
        unpack_kernel,
        out_shape=jax.ShapeDtypeStruct((8, 4, N_Y * N_IN, 2 * LANES), jnp.bfloat16),
        in_specs=[VMEM],
        out_specs=VMEM,
        compiler_params=PARAMS,
        name="unpack",
    )(second.reshape(2 * N_Y * 64, WIDTH))
    n_inputs = N_ZX * N_Y * N_IN
    whole = lax.all_gather(half.reshape(n_inputs, 2 * LANES), "core", axis=0, tiled=False)
    rows = n_inputs // N_TB
    cols = 256
    row_start = ((lax.axis_index("yhi") * 2 + lax.axis_index("core")) * rows).astype(jnp.int32).reshape(1)
    scale = np.float32(1.0 / (N_FR * N_TB))
    return pl.pallas_call(
        lambda *refs: correlate_kernel(scale, *refs),
        grid=(n_inputs // cols,),
        out_shape=jax.ShapeDtypeStruct((2, 1, rows, n_inputs), jnp.float32),
        in_specs=[pl.BlockSpec(memory_space=pltpu.SMEM), VMEM],
        out_specs=pl.BlockSpec((2, 1, rows, cols), lambda j: (0, 0, 0, j)),
        compiler_params=PARAMS,
        name="correlate",
    )(row_start, whole)


def solution(mesh):
    fine = Mesh(mesh.devices.reshape(8, 4, 4, 2, 2), ("z", "x", "ylo", "yhi", "core"))
    in_specs = (P(("z", "x", "ylo"), ("yhi", "core")), P())
    out_specs = P(None, ("z", "x", "ylo"), ("yhi", "core"), None)
    return jax.shard_map(
        per_device, mesh=fine, in_specs=in_specs, out_specs=out_specs, check_vma=False
    )
```

time: 114 us -> 87.5 us (0.77)
  local copies, waits for them, and re-layouts: 37.5 us -> 5.77 us
  blocking collectives: 15.7 us -> 35.7 us
  starting transfers between devices: 26.2 us -> 8.83 us
  between operations: 0.12 us -> 13.4 us
  waiting for transfers between devices: 24.7 us -> 17.7 us
  other arithmetic: 6.15 us -> 0 us
  Pallas kernels: 0 us -> 5.66 us
  matrix products: 2.97 us -> 0 us
    all_to_all x0 -> x2, blocking collectives: none -> 35.7 us  [the longest x1 22.6 us: per_device(): lax.all_to_all(spectra.reshape(N_ZX, N_IN, WIDTH), ('z', 'x'), 0, 0, tile...]
    all_to_all x1 -> x0, waiting for transfers between devices: 24.7 us -> none  [per_device(): lax.all_to_all(window, 'st', split_axis=0, concat_axis=1, tiled=True)]
    all_to_all x1 -> x0, starting transfers between devices: 17.4 us -> none  [per_device(): lax.all_to_all(window, 'st', split_axis=0, concat_axis=1, tiled=True)]
    reshape x2 -> x0, local copies, waits for them, and re-layouts: 17.4 us -> none  [the longest x1 16.2 us: correlate(): pairs = columns.reshape(n_ch, n_cols, length // 2, 2)]
    all_to_all x1 -> x0, local copies, waits for them, and re-layouts: 17.1 us -> none  [per_device(): lax.all_to_all(window, 'st', split_axis=0, concat_axis=1, tiled=True)]
    all_gather x0 -> x1, waiting for transfers between devices: none -> 16.1 us  [per_device(): lax.all_gather(half.reshape(n_inputs, 2 * LANES), 'core', axis=0, tiled=F...]
    all_gather x1 -> x0, blocking collectives: 15.7 us -> none  [per_device(): window = lax.all_gather(spectra, 'tb', axis=2, tiled=True)]
    pallas_call x0 -> x4, Pallas kernels: none -> 5.66 us  [the longest x1 2.6 us: per_device(): pl.pallas_call(lambda *refs: correlate_kernel(scale, *refs), grid=(n_inpu...]
  transfers between devices with their start and end apart: 2 -> 2, of which waited for: 1 -> 2; matrix products, arithmetic and copies ran while one was open for 2% -> 0% of each run, Pallas kernels for 0% -> 0%
where the time goes in v1:
time: 87.5 us; the launch traced here: 87.1 us
  blocking collectives  35.7 us (41%)
  waiting for transfers between devices  17.7 us (20%)
  between operations  13.4 us (15%)
  starting transfers between devices  8.83 us (10%)
  local copies, waits for them, and re-layouts  5.77 us (7%)
  Pallas kernels  5.66 us (6%)
    all_to_all x1, blocking collectives, per_device(): lax.all_to_all(spectra.reshape(N_ZX, N_IN, WIDTH), ('z', 'x'), 0, 0, tile...  22.6 us
    all_gather x1, waiting for transfers between devices, per_device(): lax.all_gather(half.reshape(n_inputs, 2 * LANES), 'core', axis=0, tiled=F...  16.1 us
    all_to_all x1, blocking collectives, per_device(): lax.all_to_all(packed.reshape(2 * N_Y, 64, WIDTH), ('yhi', 'ylo'), 0, 0,...  13.1 us
    ppermute x1, starting transfers between devices, per_device(): lax.ppermute(tail, ('yhi', 'core'), [(i, i + 1) for i in range(N_TB - 1)])  8.83 us
    unnamed x10, local copies, waits for them, and re-layouts  4.88 us
    pallas_call x1, Pallas kernels, per_device(): pl.pallas_call(lambda *refs: correlate_kernel(scale, *refs), grid=(n_inpu...  2.6 us
  transfers between devices with their start and end apart: 2, of which 2 were waited for; matrix products, arithmetic and copies ran while one was open for 0% of the time, Pallas kernels for 0%

profile of v1, /device:TPU:1, one launch (start us, length us, event | category | flops | bytes accessed | tf_op | source)
XLA Modules:
  0.0 87.1 jit_solution(12657087147032197740)
XLA Ops:
  6.5 0.0 all-gather.2.cloned.1.call-start
  6.5 0.9 %slice.3 = bf16[8,5632]{1,0:T(8,128)(2,1)S(1)} slice(bf16[8,24576]{1,0:T(8,128)(2,1)} %volt_ref.1), slice={[0:8], [18944:24576]} | slice | bytes 180224 | tf_op jit(solution)/shard_map/slice | solution.py:184
  7.4 8.8 %collective-permute-start = (bf16[8,5632]{1,0:T(8,128)(2,1)S(1)}, bf16[8,5632]{1,0:T(8,128)(2,1)S(1)}, u32[]{:S(2)}, u32[]{:S(2)}) collective-permute-start(bf16[8,5632]{1,0:T(8,128)(2,1)S(1)} %slice.3), channel_id=1, source_target_pairs={{0,1},{1,2},{2,3},{4,5},{5,6},{6,7},{8,9},{9,10},{10,11},{12,13},{... | collective-permute-start | bytes 270344 | tf_op jit(solution)/shard_map/ppermute | solution.py:185
  16.3 1.5 %collective-permute-done.halo_ref = bf16[8,5632]{1,0:T(8,128)(2,1)S(1)} collective-permute-done((bf16[8,5632]{1,0:T(8,128)(2,1)S(1)}, bf16[8,5632]{1,0:T(8,128)(2,1)S(1)}, u32[]{:S(2)}, u32[]{:S(2)}) %collective-permute-start) | collective-permute-done | bytes 90144 | tf_op jit(solution)/shard_map/ppermute | solution.py:185
  17.8 0.0 copy-start.1
  17.8 1.0 %copy-done.1 = bf16[8,24576]{1,0:T(8,128)(2,1)S(1)} copy-done((bf16[8,24576]{1,0:T(8,128)(2,1)S(1)}, bf16[8,24576]{1,0:T(8,128)(2,1)}, u32[]{:S(2)}) %copy-start.1) | copy-done | bytes 393240
  18.8 0.0 copy-start.2
  18.8 0.9 %copy-done.2 = bf16[256,512]{1,0:T(8,128)(2,1)S(1)} copy-done((bf16[256,512]{1,0:T(8,128)(2,1)S(1)}, bf16[256,512]{1,0:T(8,128)(2,1)}, u32[]{:S(2)}) %copy-start.2) | copy-done | bytes 262168
  19.8 0.0 copy-start.3
  19.8 0.9 %copy-done.3 = bf16[256,512]{1,0:T(8,128)(2,1)S(1)} copy-done((bf16[256,512]{1,0:T(8,128)(2,1)S(1)}, bf16[256,512]{1,0:T(8,128)(2,1)}, u32[]{:S(2)}) %copy-start.3) | copy-done | bytes 262168
  20.7 0.0 copy-start.4
  20.7 0.8 copy-done.4
  21.5 1.7 %channelize.1 = bf16[256,384]{1,0:T(8,128)(2,1)S(1)} custom-call(bf16[8,5632]{1,0:T(8,128)(2,1)S(1)} %collective-permute-done.halo_ref, bf16[8,24576]{1,0:T(8,128)(2,1)S(1)} %copy-done.1, f32[12,512]{1,0:T(8,128)S(1)} %copy-done.4, bf16[256,512]{1,0:T(8,128)(2,1)S(1)} %copy-done.3, bf16[256,512]{1,0:T(8,128)(2,1)S(1)} %copy-done.2), custom_call_target="tpu_custom_call" | custom-call | tf_op jit(solution)/shard_map/channelize/pallas_call | solution.py:187
  23.2 22.6 %all_to_all.10 = bf16[32,8,384]{2,1,0:T(8,128)(2,1)S(1)} all-to-all(bf16[32,8,384]{2,1,0:T(8,128)(2,1)S(1)} %bitcast.8), channel_id=1, replica_groups=mesh['z'=8,'x'=4,'ylo'=4,'yhi'=2,'core'=2] {'z','x'}, dimensions={0} | all-to-all | bytes 393216 | tf_op jit(solution)/shard_map/all_to_all | solution.py:201
  45.8 0.1 repack.1
  45.9 13.1 %all_to_all.11 = bf16[8,64,384]{2,1,0:T(8,128)(2,1)S(1)} all-to-all(bf16[8,64,384]{2,1,0:T(8,128)(2,1)S(1)} %bitcast.6), channel_id=1, replica_groups=mesh['z'=8,'x'=4,'ylo'=4,'yhi'=2,'core'=2] {'yhi','ylo'}, dimensions={0} | all-to-all | bytes 786432 | tf_op jit(solution)/shard_map/all_to_all | solution.py:210
  59.1 1.2 %unpack.1 = bf16[8,4,32,256]{3,2,1,0:T(8,128)(2,1)} custom-call(bf16[512,384]{1,0:T(8,128)(2,1)S(1)} %bitcast.7), custom_call_target="tpu_custom_call" | custom-call | tf_op jit(solution)/shard_map/unpack/pallas_call | solution.py:211
  60.2 0.0 all-gather.2.cloned.1.call-update
  60.3 16.1 %all-gather.2.cloned.1.call-done.refs_1_ = bf16[2,1024,256]{2,1,0:T(8,128)(2,1)} async-done(((bf16[1,1024,256]{2,1,0:T(8,128)(2,1)}), bf16[2,1024,256]{2,1,0:T(8,128)(2,1)}) %all-gather.2.cloned.1.call-update) | async-done | bytes 1048592 | tf_op jit(solution)/shard_map/all_gather | solution.py:220
  76.4 0.0 copy-start
  76.4 1.2 %copy-done = bf16[2,1024,256]{2,1,0:T(8,128)(2,1)S(1)} copy-done((bf16[2,1024,256]{2,1,0:T(8,128)(2,1)S(1)}, bf16[2,1024,256]{2,1,0:T(8,128)(2,1)}, u32[]{:S(2)}) %copy-start) | copy-done | bytes 1048600
  77.6 2.6 %correlate.1 = f32[2,1,256,1024]{3,2,1,0:T(8,128)} custom-call(s32[1]{0:T(128)} %bitcast.refs_0_, bf16[2,1024,256]{2,1,0:T(8,128)(2,1)S(1)} %copy-done), custom_call_target="tpu_custom_call" | custom-call | tf_op jit(solution)/shard_map/correlate/pallas_call | solution.py:225
Async XLA Ops:
  6.5 69.9 %all-gather.2.cloned.1.call-start = ((), (), s32[]{:S(2)}) async-start(), calls=%async_computation.2 | async-start | bytes 1572864 | tf_op jit(solution)/shard_map/all_gather | solution.py:220
  7.4 10.4 %collective-permute-start = (bf16[8,5632]{1,0:T(8,128)(2,1)S(1)}, bf16[8,5632]{1,0:T(8,128)(2,1)S(1)}, u32[]{:S(2)}, u32[]{:S(2)}) collective-permute-start(bf16[8,5632]{1,0:T(8,128)(2,1)S(1)} %slice.3), channel_id=1, source_target_pairs={{0,1},{1,2},{2,3},{4,5},{5,6},{6,7},{8,9},{9,10},{10,11},{12,13},{... | collective-permute-start | bytes 270344 | tf_op jit(solution)/shard_map/ppermute | solution.py:185
  17.8 1.0 %copy-start.1 = (bf16[8,24576]{1,0:T(8,128)(2,1)S(1)}, bf16[8,24576]{1,0:T(8,128)(2,1)}, u32[]{:S(2)}) copy-start(bf16[8,24576]{1,0:T(8,128)(2,1)} %volt_ref.1) | copy-start | bytes 1179652
  18.8 0.9 %copy-start.2 = (bf16[256,512]{1,0:T(8,128)(2,1)S(1)}, bf16[256,512]{1,0:T(8,128)(2,1)}, u32[]{:S(2)}) copy-start(bf16[256,512]{1,0:T(8,128)(2,1)} %constant.15.clone.low_ref) | copy-start | bytes 786436
  19.8 0.9 %copy-start.3 = (bf16[256,512]{1,0:T(8,128)(2,1)S(1)}, bf16[256,512]{1,0:T(8,128)(2,1)}, u32[]{:S(2)}) copy-start(bf16[256,512]{1,0:T(8,128)(2,1)} %constant.14.clone.high_ref) | copy-start | bytes 786436
  20.7 0.8 copy-start.4
  76.4 1.2 %copy-start = (bf16[2,1024,256]{2,1,0:T(8,128)(2,1)S(1)}, bf16[2,1024,256]{2,1,0:T(8,128)(2,1)}, u32[]{:S(2)}) copy-start(bf16[2,1024,256]{2,1,0:T(8,128)(2,1)} %all-gather.2.cloned.1.call-done.refs_1_) | copy-start | bytes 3145732
Sparse Core Ops, SparseCore 0:
  60.4 15.9 all-gather.1

commit v2 on v0

v2 whole, which is shorter than its diff:
```python
import math

import jax
import jax.numpy as jnp
import numpy as np
from jax import lax
from jax.experimental import pallas as pl
from jax.experimental.pallas import tpu as pltpu
from jax.sharding import Mesh
from jax.sharding import PartitionSpec as P

CH = 128
OFFSET = 64
FRAME = 512
TAPS = 12
MARGIN = TAPS - 1
N_IN = 8
N_FR = 48
N_TB = 4
SLOTS = N_FR + MARGIN
HALF = 64
LANES = 128
N_INPUTS = 1024
SWAP = [(0, 1), (1, 0)]
VMEM = pl.BlockSpec(memory_space=pltpu.VMEM)
SMEM = pl.BlockSpec(memory_space=pltpu.SMEM)
PARAMS = pltpu.CompilerParams(vmem_limit_bytes=40 * 1024 * 1024)

LOW_SLOT = N_FR - MARGIN
HIGH_SLOT = N_FR


def dft_tables():
    phase = (np.arange(CH)[:, None] + OFFSET) * np.arange(FRAME)[None, :] % FRAME
    angle = phase * (2.0 * math.pi / FRAME)
    table = np.concatenate([np.cos(angle), -np.sin(angle)], 0) / math.sqrt(FRAME)
    high = table.astype(jnp.bfloat16)
    low = (table - high.astype(np.float64)).astype(jnp.bfloat16)
    return high, low


def dot_t(a, b):
    return lax.dot_general(a, b, (((1,), (1,)), ((), ())), preferred_element_type=jnp.float32)


def lane_ids(rows):
    return lax.broadcasted_iota(jnp.int32, (rows, LANES), 1)


def channelize_kernel(
    place_ref, volt_ref, other_ref, taps_ref, high_ref, low_ref, out_ref, frames, filt, fhigh, flow, spread
):
    core, yhi = place_ref[0], place_ref[1]
    edge = MARGIN * FRAME
    own = N_FR * FRAME
    nothing = jnp.zeros((N_IN, edge), jnp.bfloat16)

    @pl.when(core == 0)
    def _():
        frames[:, :edge] = nothing
        frames[:, edge : edge + own] = volt_ref[...]
        frames[:, edge + own :] = other_ref[:, :edge]

    @pl.when(core == 1)
    def _():
        frames[:, :own] = volt_ref[...]

    @pl.when((core == 1) & (yhi == 0))
    def _():
        frames[:, own : own + edge] = volt_ref[:, own - edge :]
        frames[:, own + edge :] = nothing

    @pl.when((core == 1) & (yhi == 1))
    def _():
        frames[:, own : own + edge] = nothing
        frames[:, own + edge :] = other_ref[:, :edge]

    @pl.loop(0, FRAME // LANES)
    def _(block):
        lo = pl.multiple_of(block * LANES, LANES)
        taps = [jnp.broadcast_to(taps_ref[k : k + 1, pl.ds(lo, LANES)], (N_IN, LANES)) for k in range(TAPS)]
        window = []
        for t in range(SLOTS + MARGIN):
            window.append(frames[:, pl.ds(pl.multiple_of(t * FRAME + lo, LANES), LANES)].astype(jnp.float32))
            if t < MARGIN:
                continue
            total = taps[0] * window[0]
            for k in range(1, TAPS):
                total = total + taps[k] * window[k]
            window.pop(0)
            f = t - MARGIN
            filt[block, f * N_IN : (f + 1) * N_IN, :] = total
        filt[block, SLOTS * N_IN :, :] = jnp.zeros(((HALF - SLOTS) * N_IN, LANES), jnp.float32)

    for i in range(N_IN):
        for block in range(FRAME // LANES):
            x = filt[block, pl.ds(i, HALF, stride=N_IN), :]
            high = x.astype(jnp.bfloat16)
            low = (x - high.astype(jnp.float32)).astype(jnp.bfloat16)
            fhigh[i * HALF : (i + 1) * HALF, block * LANES : (block + 1) * LANES] = high
            flow[i * HALF : (i + 1) * HALF, block * LANES : (block + 1) * LANES] = low

    lanes = lane_ids(CH)
    slot = lanes % HALF
    drop = (slot < MARGIN) & (core == 0) & (yhi == 1)
    split = (slot >= LOW_SLOT) & (slot < HIGH_SLOT) & (core == 1)
    for pair in range(N_IN // 2):
        fh = fhigh[pair * LANES : (pair + 1) * LANES, :]
        fl = flow[pair * LANES : (pair + 1) * LANES, :]
        spec = dot_t(high_ref[...], fh) + (dot_t(high_ref[...], fl) + dot_t(low_ref[...], fh))
        real, imag = spec[:CH], spec[CH:]
        first = jnp.where(lanes < HALF, real, pltpu.roll(imag, HALF, 1))
        second = jnp.where(lanes < HALF, pltpu.roll(real, HALF, 1), imag)
        for sub, value in enumerate((first, second)):
            rest = value - value.astype(jnp.bfloat16).astype(jnp.float32)
            value = jnp.where(split, pltpu.roll(rest, LANES - MARGIN, 1), value)
            value = jnp.where(drop, 0.0, value)
            spread[pl.ds(pair * 2 + sub, CH, stride=N_IN), :] = value
    out_ref[...] = spread[...].astype(jnp.bfloat16)


def correlate_kernel(scale, place_ref, own_ref, far_ref, near_ref, cross_ref, out_ref, cols_ref, rows_ref):
    core, yhi = place_ref[0], place_ref[1]
    rows = out_ref.shape[2]
    cols = out_ref.shape[3]

    def lay(plain, parts):
        cols_ref[:, :LANES] = plain[0][...]
        cols_ref[:, LANES : 2 * LANES] = plain[1][...]
        slot = lane_ids(N_INPUTS) % HALF
        edge = (slot >= HIGH_SLOT) & (slot < SLOTS)
        low = (slot >= LOW_SLOT) & (slot < HIGH_SLOT)
        a, b = parts[0][...].astype(jnp.float32), parts[1][...].astype(jnp.float32)
        total = (a + pltpu.roll(a, MARGIN, 1)) + (b + pltpu.roll(b, MARGIN, 1))
        one = jnp.where(edge, total, jnp.where(low, 0.0, a))
        two = jnp.where(edge | low, 0.0, b)
        cols_ref[:, 2 * LANES : 3 * LANES] = one.astype(jnp.bfloat16)
        cols_ref[:, 3 * LANES :] = two.astype(jnp.bfloat16)

    @pl.when(pl.program_id(0) == 0)
    def _():
        @pl.when(core == 0)
        def _():
            lay((own_ref, far_ref), (near_ref, cross_ref))

        @pl.when(core == 1)
        def _():
            lay((near_ref, cross_ref), (own_ref, far_ref))

        own = pl.multiple_of((yhi * 2 + core) * rows, rows)
        lanes = lane_ids(rows)
        for t in range(N_TB):
            x = cols_ref[pl.ds(own, rows), t * LANES : (t + 1) * LANES]
            rows_ref[0, :, t * LANES : (t + 1) * LANES] = x
            turned = pltpu.roll(x.astype(jnp.float32), HALF, 1)
            turned = jnp.where(lanes < HALF, turned, -turned)
            rows_ref[1, :, t * LANES : (t + 1) * LANES] = turned.astype(jnp.bfloat16)

    col = pl.multiple_of(pl.program_id(0) * cols, cols)
    b = cols_ref[pl.ds(col, cols), :]
    out_ref[0, 0] = dot_t(rows_ref[0], b) * scale
    out_ref[1, 0] = dot_t(rows_ref[1], b) * scale


def per_device(voltages, fir_taps):
    place = jnp.stack([lax.axis_index("core"), lax.axis_index("yhi")]).astype(jnp.int32)
    other = lax.ppermute(voltages, "core", SWAP)
    high, low = dft_tables()
    spectra = pl.pallas_call(
        channelize_kernel,
        out_shape=jax.ShapeDtypeStruct((CH * N_IN, LANES), jnp.bfloat16),
        in_specs=[SMEM] + [VMEM] * 5,
        out_specs=VMEM,
        scratch_shapes=[
            pltpu.VMEM((N_IN, (SLOTS + MARGIN) * FRAME), jnp.bfloat16),
            pltpu.VMEM((FRAME // LANES, HALF * N_IN, LANES), jnp.float32),
            pltpu.VMEM((HALF * N_IN, FRAME), jnp.bfloat16),
            pltpu.VMEM((HALF * N_IN, FRAME), jnp.bfloat16),
            pltpu.VMEM((CH * N_IN, LANES), jnp.float32),
        ],
        compiler_params=PARAMS,
        name="channelize",
    )(place, voltages, other, fir_taps, jnp.asarray(high), jnp.asarray(low))
    turned = lax.all_to_all(spectra.reshape(CH, N_IN, LANES), ("z", "x", "ylo"), 0, 0, tiled=True)
    own = turned.reshape(N_INPUTS, LANES)
    far = lax.ppermute(own, "yhi", SWAP)
    near = lax.ppermute(own, "core", SWAP)
    cross = lax.ppermute(far, "core", SWAP)
    rows = N_INPUTS // N_TB
    cols = 256
    scale = np.float32(1.0 / (N_FR * N_TB))
    return pl.pallas_call(
        lambda *refs: correlate_kernel(scale, *refs),
        grid=(N_INPUTS // cols,),
        out_shape=jax.ShapeDtypeStruct((2, 1, rows, N_INPUTS), jnp.float32),
        in_specs=[SMEM] + [VMEM] * 4,
        out_specs=pl.BlockSpec((2, 1, rows, cols), lambda j: (0, 0, 0, j)),
        scratch_shapes=[
            pltpu.VMEM((N_INPUTS, N_TB * LANES), jnp.bfloat16),
            pltpu.VMEM((2, rows, N_TB * LANES), jnp.bfloat16),
        ],
        compiler_params=PARAMS,
        name="correlate",
    )(place, own, far, near, cross)


def solution(mesh):
    fine = Mesh(mesh.devices.reshape(8, 4, 4, 2, 2), ("z", "x", "ylo", "yhi", "core"))
    in_specs = (P(("z", "x", "ylo"), ("yhi", "core")), P())
    out_specs = P(None, ("z", "x", "ylo"), ("yhi", "core"), None)
    return jax.shard_map(
        per_device, mesh=fine, in_specs=in_specs, out_specs=out_specs, check_vma=False
    )
```

time: 114 us -> 67.2 us (0.59)
  the two profiles are of different devices: /device:TPU:1 before, /device:TPU:57 now
where the time goes in v2:
time: 67.2 us; the launch traced here: 66.8 us
  blocking collectives  29.6 us (44%)
  waiting for transfers between devices  14 us (21%)
  starting transfers between devices  13.2 us (20%)
  Pallas kernels  6.31 us (9%)
  local copies, waits for them, and re-layouts  3.65 us (5%)
    all_to_all x1, blocking collectives, per_device(): lax.all_to_all(spectra.reshape(CH, N_IN, LANES), ('z', 'x', 'ylo'), 0, 0,...  29.6 us
    ppermute x1, waiting for transfers between devices, per_device(): far = lax.ppermute(own, 'yhi', SWAP)  11.4 us
    ppermute x1, starting transfers between devices, per_device(): far = lax.ppermute(own, 'yhi', SWAP)  4.43 us
    pallas_call x1, Pallas kernels, per_device(): pl.pallas_call(lambda *refs: correlate_kernel(scale, *refs), grid=(N_INPU...  3.67 us
    unnamed x8, local copies, waits for them, and re-layouts  3.65 us
    ppermute x1, starting transfers between devices, per_device(): near = lax.ppermute(own, 'core', SWAP)  3.34 us
    ppermute x1, starting transfers between devices, per_device(): cross = lax.ppermute(far, 'core', SWAP)  2.81 us
    pallas_call x1, Pallas kernels, per_device(): pl.pallas_call(channelize_kernel, out_shape=jax.ShapeDtypeStruct((CH * N_...  2.64 us
  transfers between devices with their start and end apart: 4, of which 3 were waited for; matrix products, arithmetic and copies ran while one was open for 0% of the time, Pallas kernels for 0%

profile of v2, /device:TPU:57, one launch (start us, length us, event | category | flops | bytes accessed | tf_op | source)
XLA Modules:
  0.0 66.8 jit_solution(15329246622049618219)
XLA Ops:
  0.0 2.6 %collective-permute-start = (bf16[8,24576]{1,0:T(8,128)(2,1)}, bf16[8,24576]{1,0:T(8,128)(2,1)S(1)}, u32[]{:S(2)}, u32[]{:S(2)}) collective-permute-start(bf16[8,24576]{1,0:T(8,128)(2,1)} %volt_ref.1), channel_id=1, source_target_pairs={{0,1},{1,0},{2,3},{3,2},{4,5},{5,4},{6,7},{7,6},{8,9},{9,8},{10,11... | collective-permute-start | bytes 1179656 | tf_op jit(solution)/shard_map/ppermute | solution.py:167
  2.6 0.1 pad_add_fusion.place_ref.refs_0_
  2.7 1.5 %collective-permute-done.other_ref = bf16[8,24576]{1,0:T(8,128)(2,1)S(1)} collective-permute-done((bf16[8,24576]{1,0:T(8,128)(2,1)}, bf16[8,24576]{1,0:T(8,128)(2,1)S(1)}, u32[]{:S(2)}, u32[]{:S(2)}) %collective-permute-start) | collective-permute-done | bytes 393248 | tf_op jit(solution)/shard_map/ppermute | solution.py:167
  4.1 0.0 copy-start
  4.1 1.0 %copy-done = bf16[8,24576]{1,0:T(8,128)(2,1)S(1)} copy-done((bf16[8,24576]{1,0:T(8,128)(2,1)S(1)}, bf16[8,24576]{1,0:T(8,128)(2,1)}, u32[]{:S(2)}) %copy-start) | copy-done | bytes 393240
  5.1 0.0 copy-start.1
  5.1 0.9 %copy-done.1 = bf16[256,512]{1,0:T(8,128)(2,1)S(1)} copy-done((bf16[256,512]{1,0:T(8,128)(2,1)S(1)}, bf16[256,512]{1,0:T(8,128)(2,1)}, u32[]{:S(2)}) %copy-start.1) | copy-done | bytes 262168
  6.1 0.0 copy-start.2
  6.1 0.9 %copy-done.2 = bf16[256,512]{1,0:T(8,128)(2,1)S(1)} copy-done((bf16[256,512]{1,0:T(8,128)(2,1)S(1)}, bf16[256,512]{1,0:T(8,128)(2,1)}, u32[]{:S(2)}) %copy-start.2) | copy-done | bytes 262168
  7.0 0.0 copy-start.3
  7.0 0.8 %copy-done.3 = f32[12,512]{1,0:T(8,128)S(1)} copy-done((f32[12,512]{1,0:T(8,128)S(1)}, f32[12,512]{1,0:T(8,128)}, u32[]{:S(2)}) %copy-start.3) | copy-done | bytes 24600
  7.8 2.6 %channelize.1 = bf16[1024,128]{1,0:T(8,128)(2,1)S(1)} custom-call(s32[2]{0:T(128)S(1)} %pad_add_fusion.place_ref.refs_0_, bf16[8,24576]{1,0:T(8,128)(2,1)S(1)} %copy-done, bf16[8,24576]{1,0:T(8,128)(2,1)S(1)} %collective-permute-done.other_ref, f32[12,512]{1,0:T(8,128)S(1)} %copy-done.3, bf16[256,512]{1,0:T(8,128)(2,1)S(1)} %copy-done.2, ...), custom_call_target="tpu_custom_call" | custom-call | tf_op jit(solution)/shard_map/channelize/pallas_call | solution.py:169
  10.4 29.6 %all_to_all.5 = bf16[128,8,128]{2,1,0:T(8,128)(2,1)S(1)} all-to-all(bf16[128,8,128]{2,1,0:T(8,128)(2,1)S(1)} %bitcast.4), channel_id=1, replica_groups=mesh['z'=8,'x'=4,'ylo'=4,'yhi'=2,'core'=2] {'z','x','ylo'}, dimensions={0} | all-to-all | bytes 524288 | tf_op jit(solution)/shard_map/all_to_all | solution.py:184
  40.0 4.4 %collective-permute-start.1 = (bf16[1024,128]{1,0:T(8,128)(2,1)S(1)}, bf16[1024,128]{1,0:T(8,128)(2,1)S(1)}, u32[]{:S(2)}, u32[]{:S(2)}) collective-permute-start(bf16[1024,128]{1,0:T(8,128)(2,1)S(1)} %bitcast.5), channel_id=1, source_target_pairs={{0,2},{2,0},{1,3},{3,1},{4,6},{6,4},{5,7},{7,5},{8,10},{10,8},{9,1... | collective-permute-start | bytes 786440 | tf_op jit(solution)/shard_map/ppermute | solution.py:186
  44.4 3.3 %collective-permute-start.2 = (bf16[1024,128]{1,0:T(8,128)(2,1)S(1)}, bf16[1024,128]{1,0:T(8,128)(2,1)S(1)}, u32[]{:S(2)}, u32[]{:S(2)}) collective-permute-start(bf16[1024,128]{1,0:T(8,128)(2,1)S(1)} %bitcast.6), channel_id=1, source_target_pairs={{0,1},{1,0},{2,3},{3,2},{4,5},{5,4},{6,7},{7,6},{8,9},{9,8},{10,11... | collective-permute-start | bytes 786440 | tf_op jit(solution)/shard_map/ppermute | solution.py:187
  47.8 11.4 %collective-permute-done.1.refs_2_ = bf16[1024,128]{1,0:T(8,128)(2,1)S(1)} collective-permute-done((bf16[1024,128]{1,0:T(8,128)(2,1)S(1)}, bf16[1024,128]{1,0:T(8,128)(2,1)S(1)}, u32[]{:S(2)}, u32[]{:S(2)}) %collective-permute-start.1) | collective-permute-done | bytes 262176 | tf_op jit(solution)/shard_map/ppermute | solution.py:186
  59.2 2.8 %collective-permute-start.3 = (bf16[1024,128]{1,0:T(8,128)(2,1)S(1)}, bf16[1024,128]{1,0:T(8,128)(2,1)S(1)}, u32[]{:S(2)}, u32[]{:S(2)}) collective-permute-start(bf16[1024,128]{1,0:T(8,128)(2,1)S(1)} %collective-permute-done.1.refs_2_), channel_id=1, source_target_pairs={{0,1},{1,0},{2,3},{3,2},{4,5},{5,4},{6,7},{7,6},{8,9},{9,8},{10,11... | collective-permute-start | bytes 786440 | tf_op jit(solution)/shard_map/ppermute | solution.py:188
  62.0 0.0 collective-permute-done.2.refs_3_
  62.0 1.1 %collective-permute-done.3.refs_4_ = bf16[1024,128]{1,0:T(8,128)(2,1)S(1)} collective-permute-done((bf16[1024,128]{1,0:T(8,128)(2,1)S(1)}, bf16[1024,128]{1,0:T(8,128)(2,1)S(1)}, u32[]{:S(2)}, u32[]{:S(2)}) %collective-permute-start.3) | collective-permute-done | bytes 262176 | tf_op jit(solution)/shard_map/ppermute | solution.py:188
  63.2 3.7 %correlate.1 = f32[2,1,256,1024]{3,2,1,0:T(8,128)} custom-call(s32[2]{0:T(128)S(1)} %pad_add_fusion.place_ref.refs_0_, bf16[1024,128]{1,0:T(8,128)(2,1)S(1)} %bitcast.7, bf16[1024,128]{1,0:T(8,128)(2,1)S(1)} %collective-permute-done.1.refs_2_, bf16[1024,128]{1,0:T(8,128)(2,1)S(1)} %collective-permute-done.2.refs_3_, ...), custom_call_target="tpu_custom_call" | custom-call | tf_op jit(solution)/shard_map/correlate/pallas_call | solution.py:192
Async XLA Ops:
  0.0 4.1 %collective-permute-start = (bf16[8,24576]{1,0:T(8,128)(2,1)}, bf16[8,24576]{1,0:T(8,128)(2,1)S(1)}, u32[]{:S(2)}, u32[]{:S(2)}) collective-permute-start(bf16[8,24576]{1,0:T(8,128)(2,1)} %volt_ref.1), channel_id=1, source_target_pairs={{0,1},{1,0},{2,3},{3,2},{4,5},{5,4},{6,7},{7,6},{8,9},{9,8},{10,11... | collective-permute-start | bytes 1179656 | tf_op jit(solution)/shard_map/ppermute | solution.py:167
  4.1 1.0 %copy-start = (bf16[8,24576]{1,0:T(8,128)(2,1)S(1)}, bf16[8,24576]{1,0:T(8,128)(2,1)}, u32[]{:S(2)}) copy-start(bf16[8,24576]{1,0:T(8,128)(2,1)} %volt_ref.1) | copy-start | bytes 1179652
  5.1 0.9 %copy-start.1 = (bf16[256,512]{1,0:T(8,128)(2,1)S(1)}, bf16[256,512]{1,0:T(8,128)(2,1)}, u32[]{:S(2)}) copy-start(bf16[256,512]{1,0:T(8,128)(2,1)} %constant.11.clone.low_ref) | copy-start | bytes 786436
  6.1 0.9 %copy-start.2 = (bf16[256,512]{1,0:T(8,128)(2,1)S(1)}, bf16[256,512]{1,0:T(8,128)(2,1)}, u32[]{:S(2)}) copy-start(bf16[256,512]{1,0:T(8,128)(2,1)} %constant.10.clone.high_ref) | copy-start | bytes 786436
  7.0 0.8 %copy-start.3 = (f32[12,512]{1,0:T(8,128)S(1)}, f32[12,512]{1,0:T(8,128)}, u32[]{:S(2)}) copy-start(f32[12,512]{1,0:T(8,128)} %taps_ref.1) | copy-start | bytes 73732
  40.0 19.2 %collective-permute-start.1 = (bf16[1024,128]{1,0:T(8,128)(2,1)S(1)}, bf16[1024,128]{1,0:T(8,128)(2,1)S(1)}, u32[]{:S(2)}, u32[]{:S(2)}) collective-permute-start(bf16[1024,128]{1,0:T(8,128)(2,1)S(1)} %bitcast.5), channel_id=1, source_target_pairs={{0,2},{2,0},{1,3},{3,1},{4,6},{6,4},{5,7},{7,5},{8,10},{10,8},{9,1... | collective-permute-start | bytes 786440 | tf_op jit(solution)/shard_map/ppermute | solution.py:186
  44.4 17.6 %collective-permute-start.2 = (bf16[1024,128]{1,0:T(8,128)(2,1)S(1)}, bf16[1024,128]{1,0:T(8,128)(2,1)S(1)}, u32[]{:S(2)}, u32[]{:S(2)}) collective-permute-start(bf16[1024,128]{1,0:T(8,128)(2,1)S(1)} %bitcast.6), channel_id=1, source_target_pairs={{0,1},{1,0},{2,3},{3,2},{4,5},{5,4},{6,7},{7,6},{8,9},{9,8},{10,11... | collective-permute-start | bytes 786440 | tf_op jit(solution)/shard_map/ppermute | solution.py:187
  59.2 4.0 %collective-permute-start.3 = (bf16[1024,128]{1,0:T(8,128)(2,1)S(1)}, bf16[1024,128]{1,0:T(8,128)(2,1)S(1)}, u32[]{:S(2)}, u32[]{:S(2)}) collective-permute-start(bf16[1024,128]{1,0:T(8,128)(2,1)S(1)} %collective-permute-done.1.refs_2_), channel_id=1, source_target_pairs={{0,1},{1,0},{2,3},{3,2},{4,5},{5,4},{6,7},{7,6},{8,9},{9,8},{10,11... | collective-permute-start | bytes 786440 | tf_op jit(solution)/shard_map/ppermute | solution.py:188

commit v3 on v2

v3 whole, which is shorter than its diff:
```python
import math

import jax
import jax.numpy as jnp
import numpy as np
from jax import lax
from jax.experimental import pallas as pl
from jax.experimental.pallas import tpu as pltpu
from jax.sharding import Mesh
from jax.sharding import PartitionSpec as P

CH = 128
OFFSET = 64
FRAME = 512
TAPS = 12
MARGIN = TAPS - 1
N_IN = 8
N_FR = 48
N_TB = 4
SLOTS = N_FR + MARGIN
HALF = 64
LANES = 128
N_INPUTS = 1024
SWAP = [(0, 1), (1, 0)]
HBM = pl.BlockSpec(memory_space=pltpu.HBM)
VMEM = pl.BlockSpec(memory_space=pltpu.VMEM)
PARAMS = pltpu.CompilerParams(vmem_limit_bytes=40 * 1024 * 1024)

LOW_SLOT = N_FR - MARGIN
HIGH_SLOT = N_FR
SPARE = HALF - SLOTS
RIDERS = -(-SLOTS // SPARE)


def dft_tables():
    phase = (np.arange(CH)[:, None] + OFFSET) * np.arange(FRAME)[None, :] % FRAME
    angle = phase * (2.0 * math.pi / FRAME)
    table = np.concatenate([np.cos(angle), -np.sin(angle)], 0) / math.sqrt(FRAME)
    high = table.astype(jnp.bfloat16)
    low = (table - high.astype(np.float64)).astype(jnp.bfloat16)
    return high, low


def dot_t(a, b):
    return lax.dot_general(a, b, (((1,), (1,)), ((), ())), preferred_element_type=jnp.float32)


def lane_ids(rows):
    return lax.broadcasted_iota(jnp.int32, (rows, LANES), 1)


def fetch(pairs, sems):
    copies = [pltpu.make_async_copy(src, dst, sems.at[n]) for n, (src, dst) in enumerate(pairs)]
    for copy in copies:
        copy.start()
    return copies


def run_filter(taps_ref, frame_at, keep, count, block):
    lo = pl.multiple_of(block * LANES, LANES)
    taps = [jnp.broadcast_to(taps_ref[k : k + 1, pl.ds(lo, LANES)], (N_IN, LANES)) for k in range(TAPS)]
    window = []
    for t in range(count + MARGIN):
        window.append(frame_at(t, lo).astype(jnp.float32))
        if t < MARGIN:
            continue
        total = taps[0] * window[0]
        for k in range(1, TAPS):
            total = total + taps[k] * window[k]
        window.pop(0)
        keep(t - MARGIN, total)


def pieces(x):
    high = x.astype(jnp.bfloat16)
    return high, (x - high.astype(jnp.float32)).astype(jnp.bfloat16)


def at(t, lo):
    return pl.ds(pl.multiple_of(t * FRAME + lo, LANES), LANES)


def prefilter_kernel(
    volt_hbm, taps_hbm, high_hbm, low_hbm, fhigh, flow, seam, taps_ref, high_ref, low_ref, frames, filt, sems
):
    core, yhi = lax.axis_index("core"), lax.axis_index("yhi")
    edge = MARGIN * FRAME
    own = N_FR * FRAME
    nothing = jnp.zeros((N_IN, edge), jnp.bfloat16)
    offset = pl.multiple_of((1 - core) * edge, LANES)
    copies = fetch(
        [
            (volt_hbm, frames.at[:, pl.ds(offset, own)]),
            (taps_hbm, taps_ref),
            (high_hbm, high_ref),
            (low_hbm, low_ref),
        ],
        sems,
    )
    tail = pltpu.make_async_copy(volt_hbm.at[:, pl.ds(own - edge, edge)], frames.at[:, pl.ds(own, edge)], sems.at[4])
    second = (core == 1) & (yhi == 0)

    @pl.when(second)
    def _():
        tail.start()

    @pl.when(core == 0)
    def _():
        frames[:, :edge] = nothing

    @pl.when((core == 1) & (yhi == 1))
    def _():
        frames[:, own:] = nothing

    copies[0].wait()
    copies[1].wait()

    @pl.when(second)
    def _():
        tail.wait()

    seam[...] = frames[:, own:]

    @pl.loop(0, FRAME // LANES)
    def _(block):
        def keep(f, x):
            filt[block, f * N_IN : (f + 1) * N_IN, :] = x

        run_filter(taps_ref, lambda t, lo: frames[:, at(t, lo)], keep, N_FR, block)

    for i in range(N_IN):
        for block in range(FRAME // LANES):
            high, low = pieces(filt[block, pl.ds(i, N_FR, stride=N_IN), :])
            fhigh[i * N_FR : (i + 1) * N_FR, block * LANES : (block + 1) * LANES] = high
            flow[i * N_FR : (i + 1) * N_FR, block * LANES : (block + 1) * LANES] = low
    copies[2].wait()
    copies[3].wait()


def channelize_kernel(fhigh, flow, seam, other_ref, taps_ref, high_ref, low_ref, out_ref, filt, ghigh, glow, spread):
    core, yhi = lax.axis_index("core"), lax.axis_index("yhi")
    more = HALF - N_FR
    real_samples = (core == 0) | (yhi == 1)

    def frame_at(t, lo):
        if t < MARGIN:
            return seam[:, at(t, lo)]
        return jnp.where(real_samples, other_ref[:, at(t - MARGIN, lo)].astype(jnp.float32), 0.0)

    @pl.loop(0, FRAME // LANES)
    def _(block):
        def keep(f, x):
            filt[block, f * N_IN : (f + 1) * N_IN, :] = x

        run_filter(taps_ref, frame_at, keep, MARGIN, block)
        filt[block, MARGIN * N_IN :, :] = jnp.zeros(((more - MARGIN) * N_IN, LANES), jnp.float32)

    for i in range(N_IN):
        for block in range(FRAME // LANES):
            high, low = pieces(filt[block, pl.ds(i, more, stride=N_IN), :])
            ghigh[i * more : (i + 1) * more, block * LANES : (block + 1) * LANES] = high
            glow[i * more : (i + 1) * more, block * LANES : (block + 1) * LANES] = low

    lanes = lane_ids(CH)
    slot = lanes % HALF
    drop = (slot < MARGIN) & (core == 0) & (yhi == 1)
    split = (slot >= LOW_SLOT) & (slot < HIGH_SLOT) & (core == 1)

    def rows_of(f, g, i):
        return [f[i * N_FR : (i + 1) * N_FR, :], g[i * more : (i + 1) * more, :]]

    for pair in range(N_IN // 2):
        i = pair * 2
        fh = jnp.concatenate(rows_of(fhigh, ghigh, i) + rows_of(fhigh, ghigh, i + 1), 0)
        fl = jnp.concatenate(rows_of(flow, glow, i) + rows_of(flow, glow, i + 1), 0)
        spec = dot_t(high_ref[...], fh) + (dot_t(high_ref[...], fl) + dot_t(low_ref[...], fh))
        real, imag = spec[:CH], spec[CH:]
        first = jnp.where(lanes < HALF, real, pltpu.roll(imag, HALF, 1))
        second = jnp.where(lanes < HALF, pltpu.roll(real, HALF, 1), imag)
        for sub, value in enumerate((first, second)):
            rest = value - value.astype(jnp.bfloat16).astype(jnp.float32)
            value = jnp.where(split, pltpu.roll(rest, LANES - MARGIN, 1), value)
            value = jnp.where(drop, 0.0, value)
            spread[pl.ds(i + sub, CH, stride=N_IN), :] = value
    out_ref[...] = spread[...].astype(jnp.bfloat16)


def spare(lanes):
    return lanes % HALF >= SLOTS


def pack_kernel(in_ref, out_ref):
    lanes = lane_ids(N_IN)
    kept = out_ref.shape[0]
    last = in_ref[kept:, :].astype(jnp.float32)
    tiles = []
    for m in range(RIDERS):
        tile = in_ref[m * N_IN : (m + 1) * N_IN, :].astype(jnp.float32)
        tiles.append(jnp.where(spare(lanes), pltpu.roll(last, SLOTS - SPARE * m, 1), tile))
    out_ref[: RIDERS * N_IN, :] = jnp.concatenate(tiles, 0).astype(jnp.bfloat16)
    out_ref[RIDERS * N_IN :, :] = in_ref[RIDERS * N_IN : kept, :]


def unpack(ref, block):
    lanes = lane_ids(N_IN)
    slot = lanes % HALF
    carriers = ref[block, : RIDERS * N_IN, :].astype(jnp.float32)
    last = jnp.zeros((N_IN, LANES), jnp.float32)
    tiles = []
    for m in range(RIDERS):
        tile = carriers[m * N_IN : (m + 1) * N_IN]
        moved = pltpu.roll(tile, (SPARE * m - SLOTS) % LANES, 1)
        last = jnp.where((slot >= SPARE * m) & (slot < SPARE * (m + 1)), moved, last)
        tiles.append(jnp.where(spare(lanes), 0.0, tile))
    last = jnp.where(spare(lanes), 0.0, last)
    rest = ref[block, RIDERS * N_IN :, :].astype(jnp.float32)
    return jnp.concatenate(tiles + [rest, last], 0)


def correlate_kernel(scale, all_ref, out_hbm, cols_ref, rows_ref, out_ref, sems):
    core, yhi = lax.axis_index("core"), lax.axis_index("yhi")
    chunks, _, rows, cols = out_ref.shape
    cols_ref[:, :LANES] = unpack(all_ref, 0).astype(jnp.bfloat16)
    cols_ref[:, LANES : 2 * LANES] = unpack(all_ref, 2).astype(jnp.bfloat16)
    slot = lane_ids(N_INPUTS) % HALF
    edge = (slot >= HIGH_SLOT) & (slot < SLOTS)
    low = (slot >= LOW_SLOT) & (slot < HIGH_SLOT)
    a, b = unpack(all_ref, 1), unpack(all_ref, 3)
    total = (a + pltpu.roll(a, MARGIN, 1)) + (b + pltpu.roll(b, MARGIN, 1))
    one = jnp.where(edge, total, jnp.where(low, 0.0, a))
    two = jnp.where(edge | low, 0.0, b)
    cols_ref[:, 2 * LANES : 3 * LANES] = one.astype(jnp.bfloat16)
    cols_ref[:, 3 * LANES :] = two.astype(jnp.bfloat16)

    own = pl.multiple_of((yhi * 2 + core) * rows, rows)
    lanes = lane_ids(rows)
    for t in range(N_TB):
        x = cols_ref[pl.ds(own, rows), t * LANES : (t + 1) * LANES]
        rows_ref[0, :, t * LANES : (t + 1) * LANES] = x
        turned = pltpu.roll(x.astype(jnp.float32), HALF, 1)
        turned = jnp.where(lanes < HALF, turned, -turned)
        rows_ref[1, :, t * LANES : (t + 1) * LANES] = turned.astype(jnp.bfloat16)

    copies = []
    for j in range(chunks):
        cut = slice(j * cols, (j + 1) * cols)
        for part in range(2):
            out_ref[j, part] = dot_t(rows_ref[part], cols_ref[cut, :]) * scale
            copy = pltpu.make_async_copy(out_ref.at[j, part], out_hbm.at[part, 0, :, cut], sems.at[j, part])
            copy.start()
            copies.append(copy)
    for copy in copies:
        copy.wait()


def far_memory(x):
    return pltpu.with_memory_space_constraint(x, pltpu.HBM)


def per_device(voltages, fir_taps):
    other = lax.ppermute(voltages, "core", SWAP)
    high, low = (jnp.asarray(table) for table in dft_tables())
    seam_shape = (N_IN, MARGIN * FRAME)
    fhigh, flow, seam, taps, high, low = pl.pallas_call(
        prefilter_kernel,
        out_shape=[
            jax.ShapeDtypeStruct((N_IN * N_FR, FRAME), jnp.bfloat16),
            jax.ShapeDtypeStruct((N_IN * N_FR, FRAME), jnp.bfloat16),
            jax.ShapeDtypeStruct(seam_shape, jnp.bfloat16),
            jax.ShapeDtypeStruct(fir_taps.shape, jnp.float32),
            jax.ShapeDtypeStruct(high.shape, jnp.bfloat16),
            jax.ShapeDtypeStruct(low.shape, jnp.bfloat16),
        ],
        in_specs=[HBM] * 4,
        out_specs=[VMEM] * 6,
        scratch_shapes=[
            pltpu.VMEM((N_IN, SLOTS * FRAME), jnp.bfloat16),
            pltpu.VMEM((FRAME // LANES, N_FR * N_IN, LANES), jnp.float32),
            pltpu.SemaphoreType.DMA((5,)),
        ],
        compiler_params=PARAMS,
        cost_estimate=pl.CostEstimate(flops=10**8, bytes_accessed=4 * 10**6, transcendentals=0),
        name="prefilter",
    )(*(far_memory(x) for x in (voltages, fir_taps, high, low)))
    more = HALF - N_FR
    spectra = pl.pallas_call(
        channelize_kernel,
        out_shape=jax.ShapeDtypeStruct((CH * N_IN, LANES), jnp.bfloat16),
        in_specs=[VMEM] * 7,
        out_specs=VMEM,
        scratch_shapes=[
            pltpu.VMEM((FRAME // LANES, more * N_IN, LANES), jnp.float32),
            pltpu.VMEM((more * N_IN, FRAME), jnp.bfloat16),
            pltpu.VMEM((more * N_IN, FRAME), jnp.bfloat16),
            pltpu.VMEM((CH * N_IN, LANES), jnp.float32),
        ],
        compiler_params=PARAMS,
        name="channelize",
    )(fhigh, flow, seam, other, taps, high, low)
    turned = lax.all_to_all(spectra.reshape(CH, N_IN, LANES), ("z", "x", "ylo"), 0, 0, tiled=True)
    packed = pl.pallas_call(
        pack_kernel,
        out_shape=jax.ShapeDtypeStruct((N_INPUTS - N_IN, LANES), jnp.bfloat16),
        in_specs=[VMEM],
        out_specs=VMEM,
        compiler_params=PARAMS,
        name="pack",
    )(turned.reshape(N_INPUTS, LANES))
    blocks = lax.all_gather(packed, ("yhi", "core"), axis=0, tiled=False)
    rows = N_INPUTS // N_TB
    cols = 256
    scale = np.float32(1.0 / (N_FR * N_TB))
    return pl.pallas_call(
        lambda *refs: correlate_kernel(scale, *refs),
        out_shape=jax.ShapeDtypeStruct((2, 1, rows, N_INPUTS), jnp.float32),
        in_specs=[VMEM],
        out_specs=HBM,
        scratch_shapes=[
            pltpu.VMEM((N_INPUTS, N_TB * LANES), jnp.bfloat16),
            pltpu.VMEM((2, rows, N_TB * LANES), jnp.bfloat16),
            pltpu.VMEM((N_INPUTS // cols, 2, rows, cols), jnp.float32),
            pltpu.SemaphoreType.DMA((N_INPUTS // cols, 2)),
        ],
        compiler_params=PARAMS,
        name="correlate",
    )(blocks)


def solution(mesh):
    fine = Mesh(mesh.devices.reshape(8, 4, 4, 2, 2), ("z", "x", "ylo", "yhi", "core"))
    in_specs = (P(("z", "x", "ylo"), ("yhi", "core")), P())
    out_specs = P(None, ("z", "x", "ylo"), ("yhi", "core"), None)
    return jax.shard_map(
        per_device, mesh=fine, in_specs=in_specs, out_specs=out_specs, check_vma=False
    )
```

time: 67.2 us -> 60.9 us (0.906)
  the two profiles are of different devices: /device:TPU:57 before, /device:TPU:1 now
where the time goes in v3:
time: 60.9 us; the launch traced here: 60.7 us
  blocking collectives  46.3 us (76%)
  starting transfers between devices  8.77 us (14%)
  Pallas kernels  5.65 us (9%)
    all_to_all x1, blocking collectives, per_device(): lax.all_to_all(spectra.reshape(CH, N_IN, LANES), ('z', 'x', 'ylo'), 0, 0,...  26.6 us
    all_gather x1, blocking collectives, per_device(): blocks = lax.all_gather(packed, ('yhi', 'core'), axis=0, tiled=False)  19.6 us
    ppermute x1, starting transfers between devices, per_device(): other = lax.ppermute(voltages, 'core', SWAP)  8.77 us
    pallas_call x1, Pallas kernels, per_device(): pl.pallas_call(prefilter_kernel, out_shape=[jax.ShapeDtypeStruct((N_IN *...  2.11 us
    pallas_call x1, Pallas kernels, per_device(): pl.pallas_call(lambda *refs: correlate_kernel(scale, *refs), out_shape=ja...  2.08 us
    pallas_call x1, Pallas kernels, per_device(): pl.pallas_call(channelize_kernel, out_shape=jax.ShapeDtypeStruct((CH * N_...  1.38 us
  transfers between devices with their start and end apart: 1, of which 0 were waited for; matrix products, arithmetic and copies ran while one was open for 0% of the time, Pallas kernels for 3%

profile of v3, /device:TPU:1, one launch (start us, length us, event | category | flops | bytes accessed | tf_op | source)
XLA Modules:
  0.0 60.7 jit_solution(2281120163473053383)
XLA Ops:
  0.0 8.8 %collective-permute-start = (bf16[8,24576]{1,0:T(8,128)(2,1)}, bf16[8,24576]{1,0:T(8,128)(2,1)S(1)}, u32[]{:S(2)}, u32[]{:S(2)}) collective-permute-start(bf16[8,24576]{1,0:T(8,128)(2,1)} %volt_hbm.1), channel_id=1, source_target_pairs={{0,1},{1,0},{2,3},{3,2},{4,5},{5,4},{6,7},{7,6},{8,9},{9,8},{10,11... | collective-permute-start | bytes 1179656 | tf_op jit(solution)/shard_map/ppermute | solution.py:261
  8.8 2.1 %prefilter.1 = (bf16[384,512]{1,0:T(8,128)(2,1)S(1)}, bf16[384,512]{1,0:T(8,128)(2,1)S(1)}, bf16[8,5632]{1,0:T(8,128)(2,1)S(1)}, f32[12,512]{1,0:T(8,128)S(1)}, ...) custom-call(bf16[8,24576]{1,0:T(8,128)(2,1)} %volt_hbm.1, f32[12,512]{1,0:T(8,128)} %taps_hbm.1, ...), custom_call_target="tpu_custom_call" | custom-call | flops 100000000 | bytes 4000000 | tf_op jit(solution)/shard_map/prefilter/pallas_call | solution.py:264
  10.9 0.0 collective-permute-done.other_ref
  10.9 1.4 %channelize.1 = bf16[1024,128]{1,0:T(8,128)(2,1)S(1)} custom-call(bf16[384,512]{1,0:T(8,128)(2,1)S(1)} %get-tuple-element.11.fhigh, bf16[384,512]{1,0:T(8,128)(2,1)S(1)} %get-tuple-element.12.flow, bf16[8,5632]{1,0:T(8,128)(2,1)S(1)} %get-tuple-element.13.seam, bf16[8,24576]{1,0:T(8,128)(2,1)S(1)} %collective-permute-done.other_ref, ...), custom_call_target="tpu_custom_call" | custom-call | tf_op jit(solution)/shard_map/channelize/pallas_call | solution.py:286
  12.3 26.6 %all_to_all.5 = bf16[128,8,128]{2,1,0:T(8,128)(2,1)S(1)} all-to-all(bf16[128,8,128]{2,1,0:T(8,128)(2,1)S(1)} %bitcast.5), channel_id=1, replica_groups=mesh['z'=8,'x'=4,'ylo'=4,'yhi'=2,'core'=2] {'z','x','ylo'}, dimensions={0} | all-to-all | bytes 524288 | tf_op jit(solution)/shard_map/all_to_all | solution.py:300
  38.9 0.1 pack.1
  39.0 19.6 %all-gather = bf16[4064,128]{1,0:T(8,128)(2,1)S(1)} all-gather(bf16[1016,128]{1,0:T(8,128)(2,1)S(1)} %pack.1), channel_id=2, replica_groups=mesh['z'=8,'x'=4,'ylo'=4,'yhi'=2,'core'=2] {'yhi','core'}, dimensions={0}, use_global_device_ids=true | all-gather | bytes 1300480 | tf_op jit(solution)/shard_map/all_gather | solution.py:309
  58.6 2.1 %correlate.1 = f32[2,1,256,1024]{3,2,1,0:T(8,128)} custom-call(bf16[4,1016,128]{2,1,0:T(8,128)(2,1)S(1)} %bitcast.3), custom_call_target="tpu_custom_call" | custom-call | tf_op jit(solution)/shard_map/correlate/pallas_call | solution.py:313
Async XLA Ops:
  0.0 10.9 %collective-permute-start = (bf16[8,24576]{1,0:T(8,128)(2,1)}, bf16[8,24576]{1,0:T(8,128)(2,1)S(1)}, u32[]{:S(2)}, u32[]{:S(2)}) collective-permute-start(bf16[8,24576]{1,0:T(8,128)(2,1)} %volt_hbm.1), channel_id=1, source_target_pairs={{0,1},{1,0},{2,3},{3,2},{4,5},{5,4},{6,7},{7,6},{8,9},{9,8},{10,11... | collective-permute-start | bytes 1179656 | tf_op jit(solution)/shard_map/ppermute | solution.py:261

commit v4 on v3

--- a/solution.py
+++ b/solution.py
@@ -28,8 +28,6 @@
 
 LOW_SLOT = N_FR - MARGIN
 HIGH_SLOT = N_FR
-SPARE = HALF - SLOTS
-RIDERS = -(-SLOTS // SPARE)
 
 
 def dft_tables():
@@ -182,70 +180,59 @@
             value = jnp.where(split, pltpu.roll(rest, LANES - MARGIN, 1), value)
             value = jnp.where(drop, 0.0, value)
             spread[pl.ds(i + sub, CH, stride=N_IN), :] = value
-    out_ref[...] = spread[...].astype(jnp.bfloat16)
-
-
-def spare(lanes):
-    return lanes % HALF >= SLOTS
-
-
-def pack_kernel(in_ref, out_ref):
-    lanes = lane_ids(N_IN)
-    kept = out_ref.shape[0]
-    last = in_ref[kept:, :].astype(jnp.float32)
-    tiles = []
-    for m in range(RIDERS):
-        tile = in_ref[m * N_IN : (m + 1) * N_IN, :].astype(jnp.float32)
-        tiles.append(jnp.where(spare(lanes), pltpu.roll(last, SLOTS - SPARE * m, 1), tile))
-    out_ref[: RIDERS * N_IN, :] = jnp.concatenate(tiles, 0).astype(jnp.bfloat16)
-    out_ref[RIDERS * N_IN :, :] = in_ref[RIDERS * N_IN : kept, :]
-
-
-def unpack(ref, block):
-    lanes = lane_ids(N_IN)
-    slot = lanes % HALF
-    carriers = ref[block, : RIDERS * N_IN, :].astype(jnp.float32)
-    last = jnp.zeros((N_IN, LANES), jnp.float32)
-    tiles = []
-    for m in range(RIDERS):
-        tile = carriers[m * N_IN : (m + 1) * N_IN]
-        moved = pltpu.roll(tile, (SPARE * m - SLOTS) % LANES, 1)
-        last = jnp.where((slot >= SPARE * m) & (slot < SPARE * (m + 1)), moved, last)
-        tiles.append(jnp.where(spare(lanes), 0.0, tile))
-    last = jnp.where(spare(lanes), 0.0, last)
-    rest = ref[block, RIDERS * N_IN :, :].astype(jnp.float32)
-    return jnp.concatenate(tiles + [rest, last], 0)
-
-
-def correlate_kernel(scale, all_ref, out_hbm, cols_ref, rows_ref, out_ref, sems):
+    result = spread[...].astype(jnp.bfloat16)
+    for copy in range(2):
+        out_ref[copy * CH * N_IN : (copy + 1) * CH * N_IN, :] = result
+
+
+def lay(in_ref, cols_ref, rows_ref, parts):
     core, yhi = lax.axis_index("core"), lax.axis_index("yhi")
-    chunks, _, rows, cols = out_ref.shape
-    cols_ref[:, :LANES] = unpack(all_ref, 0).astype(jnp.bfloat16)
-    cols_ref[:, LANES : 2 * LANES] = unpack(all_ref, 2).astype(jnp.bfloat16)
-    slot = lane_ids(N_INPUTS) % HALF
-    edge = (slot >= HIGH_SLOT) & (slot < SLOTS)
-    low = (slot >= LOW_SLOT) & (slot < HIGH_SLOT)
-    a, b = unpack(all_ref, 1), unpack(all_ref, 3)
-    total = (a + pltpu.roll(a, MARGIN, 1)) + (b + pltpu.roll(b, MARGIN, 1))
-    one = jnp.where(edge, total, jnp.where(low, 0.0, a))
-    two = jnp.where(edge | low, 0.0, b)
-    cols_ref[:, 2 * LANES : 3 * LANES] = one.astype(jnp.bfloat16)
-    cols_ref[:, 3 * LANES :] = two.astype(jnp.bfloat16)
+    rows = rows_ref.shape[1]
+
+    @pl.when(jnp.logical_not(parts))
+    def _():
+        for t in range(2):
+            cols_ref[:, t * LANES : (t + 1) * LANES] = in_ref[t * N_INPUTS : (t + 1) * N_INPUTS, :]
+
+    @pl.when(parts)
+    def _():
+        slot = lane_ids(N_INPUTS) % HALF
+        edge = (slot >= HIGH_SLOT) & (slot < SLOTS)
+        low = (slot >= LOW_SLOT) & (slot < HIGH_SLOT)
+        a = in_ref[:N_INPUTS, :].astype(jnp.float32)
+        b = in_ref[N_INPUTS:, :].astype(jnp.float32)
+        total = (a + pltpu.roll(a, MARGIN, 1)) + (b + pltpu.roll(b, MARGIN, 1))
+        one = jnp.where(edge, total, jnp.where(low, 0.0, a))
+        two = jnp.where(edge | low, 0.0, b)
+        cols_ref[:, :LANES] = one.astype(jnp.bfloat16)
+        cols_ref[:, LANES:] = two.astype(jnp.bfloat16)
 
     own = pl.multiple_of((yhi * 2 + core) * rows, rows)
     lanes = lane_ids(rows)
-    for t in range(N_TB):
+    for t in range(2):
         x = cols_ref[pl.ds(own, rows), t * LANES : (t + 1) * LANES]
         rows_ref[0, :, t * LANES : (t + 1) * LANES] = x
         turned = pltpu.roll(x.astype(jnp.float32), HALF, 1)
         turned = jnp.where(lanes < HALF, turned, -turned)
         rows_ref[1, :, t * LANES : (t + 1) * LANES] = turned.astype(jnp.bfloat16)
 
+
+def first_half_kernel(in_ref, part_ref, cols_ref, rows_ref):
+    lay(in_ref, cols_ref, rows_ref, lax.axis_index("core") == 1)
+    cols = part_ref.shape[3]
+    for j in range(part_ref.shape[0]):
+        for part in range(2):
+            part_ref[j, part] = dot_t(rows_ref[part], cols_ref[j * cols : (j + 1) * cols, :])
+
+
+def second_half_kernel(scale, in_ref, part_ref, out_hbm, cols_ref, rows_ref, out_ref, sems):
+    lay(in_ref, cols_ref, rows_ref, lax.axis_index("core") == 0)
+    chunks, _, _, cols = out_ref.shape
     copies = []
     for j in range(chunks):
         cut = slice(j * cols, (j + 1) * cols)
         for part in range(2):
-            out_ref[j, part] = dot_t(rows_ref[part], cols_ref[cut, :]) * scale
+            out_ref[j, part] = (part_ref[j, part] + dot_t(rows_ref[part], cols_ref[cut, :])) * scale
             copy = pltpu.make_async_copy(out_ref.at[j, part], out_hbm.at[part, 0, :, cut], sems.at[j, part])
             copy.start()
             copies.append(copy)
@@ -285,7 +272,7 @@
     more = HALF - N_FR
     spectra = pl.pallas_call(
         channelize_kernel,
-        out_shape=jax.ShapeDtypeStruct((CH * N_IN, LANES), jnp.bfloat16),
+        out_shape=jax.ShapeDtypeStruct((2 * CH * N_IN, LANES), jnp.bfloat16),
         in_specs=[VMEM] * 7,
         out_specs=VMEM,
         scratch_shapes=[
@@ -297,33 +284,42 @@
         compiler_params=PARAMS,
         name="channelize",
     )(fhigh, flow, seam, other, taps, high, low)
-    turned = lax.all_to_all(spectra.reshape(CH, N_IN, LANES), ("z", "x", "ylo"), 0, 0, tiled=True)
-    packed = pl.pallas_call(
-        pack_kernel,
-        out_shape=jax.ShapeDtypeStruct((N_INPUTS - N_IN, LANES), jnp.bfloat16),
+    turned = lax.all_to_all(
+        spectra.reshape(2 * CH, N_IN, LANES), ("yhi", "z", "x", "ylo"), 0, 0, tiled=True
+    )
+    own = turned.reshape(2 * N_INPUTS, LANES)
+    other_core = lax.ppermute(own, "core", SWAP)
+    rows = N_INPUTS // N_TB
+    cols = 256
+    chunks = N_INPUTS // cols
+    operands = [
+        pltpu.VMEM((N_INPUTS, 2 * LANES), jnp.bfloat16),
+        pltpu.VMEM((2, rows, 2 * LANES), jnp.bfloat16),
+    ]
+    half = pl.pallas_call(
+        first_half_kernel,
+        out_shape=jax.ShapeDtypeStruct((chunks, 2, rows, cols), jnp.float32),
         in_specs=[VMEM],
         out_specs=VMEM,
+        scratch_shapes=operands,
         compiler_params=PARAMS,
-        name="pack",
-    )(turned.reshape(N_INPUTS, LANES))
-    blocks = lax.all_gather(packed, ("yhi", "core"), axis=0, tiled=False)
-    rows = N_INPUTS // N_TB
-    cols = 256
+        cost_estimate=pl.CostEstimate(flops=3 * 10**8, bytes_accessed=3 * 10**6, transcendentals=0),
+        name="first_half",
+    )(own)
     scale = np.float32(1.0 / (N_FR * N_TB))
     return pl.pallas_call(
-        lambda *refs: correlate_kernel(scale, *refs),
+        lambda *refs: second_half_kernel(scale, *refs),
         out_shape=jax.ShapeDtypeStruct((2, 1, rows, N_INPUTS), jnp.float32),
-        in_specs=[VMEM],
+        in_specs=[VMEM, VMEM],
         out_specs=HBM,
-        scratch_shapes=[
-            pltpu.VMEM((N_INPUTS, N_TB * LANES), jnp.bfloat16),
-            pltpu.VMEM((2, rows, N_TB * LANES), jnp.bfloat16),
-            pltpu.VMEM((N_INPUTS // cols, 2, rows, cols), jnp.float32),
-            pltpu.SemaphoreType.DMA((N_INPUTS // cols, 2)),
+        scratch_shapes=operands
+        + [
+            pltpu.VMEM((chunks, 2, rows, cols), jnp.float32),
+            pltpu.SemaphoreType.DMA((chunks, 2)),
         ],
         compiler_params=PARAMS,
-        name="correlate",
-    )(blocks)
+        name="second_half",
+    )(other_core, half)
 
 
 def solution(mesh):

time: 60.9 us -> 55.9 us (0.918)
  blocking collectives: 46.3 us -> 36.3 us
  starting transfers between devices: 8.77 us -> 12.7 us
  waiting for transfers between devices: 0.01 us -> 0.76 us
    all_gather x1 -> x0, blocking collectives: 19.6 us -> none  [per_device(): blocks = lax.all_gather(packed, ('yhi', 'core'), axis=0, tiled=False)]
    all_to_all x1, blocking collectives: 26.6 us -> 36.3 us  [per_device(): lax.all_to_all(spectra.reshape(2 * CH, N_IN, LANES), ('yhi', 'z', 'x', 'y...]
    ppermute x0 -> x1, starting transfers between devices: none -> 3.88 us  [per_device(): other_core = lax.ppermute(own, 'core', SWAP)]
    ppermute x0 -> x1, waiting for transfers between devices: none -> 0.76 us  [per_device(): other_core = lax.ppermute(own, 'core', SWAP)]
  transfers between devices with their start and end apart: 1 -> 2, of which waited for: 0 -> 1; matrix products, arithmetic and copies ran while one was open for 0% -> 0% of each run, Pallas kernels for 3% -> 5%
where the time goes in v4:
time: 55.9 us; the launch traced here: 55.7 us
  blocking collectives  36.3 us (65%)
  starting transfers between devices  12.7 us (23%)
  Pallas kernels  5.97 us (11%)
  waiting for transfers between devices  0.76 us (1%)
    all_to_all x1, blocking collectives, per_device(): lax.all_to_all(spectra.reshape(2 * CH, N_IN, LANES), ('yhi', 'z', 'x', 'y...  36.3 us
    ppermute x1, starting transfers between devices, per_device(): other = lax.ppermute(voltages, 'core', SWAP)  8.77 us
    ppermute x1, starting transfers between devices, per_device(): other_core = lax.ppermute(own, 'core', SWAP)  3.88 us
    pallas_call x1, Pallas kernels, per_device(): pl.pallas_call(prefilter_kernel, out_shape=[jax.ShapeDtypeStruct((N_IN *...  2.11 us
    pallas_call x1, Pallas kernels, per_device(): pl.pallas_call(lambda *refs: second_half_kernel(scale, *refs), out_shape=...  1.72 us
    pallas_call x1, Pallas kernels, per_device(): pl.pallas_call(channelize_kernel, out_shape=jax.ShapeDtypeStruct((2 * CH...  1.38 us
  transfers between devices with their start and end apart: 2, of which 1 were waited for; matrix products, arithmetic and copies ran while one was open for 0% of the time, Pallas kernels for 5%

profile of v4, /device:TPU:1, one launch (start us, length us, event | category | flops | bytes accessed | tf_op | source)
XLA Modules:
  0.0 55.7 jit_solution(3205745120240787272)
XLA Ops:
  0.0 8.8 %collective-permute-start = (bf16[8,24576]{1,0:T(8,128)(2,1)}, bf16[8,24576]{1,0:T(8,128)(2,1)S(1)}, u32[]{:S(2)}, u32[]{:S(2)}) collective-permute-start(bf16[8,24576]{1,0:T(8,128)(2,1)} %volt_hbm.1), channel_id=1, source_target_pairs={{0,1},{1,0},{2,3},{3,2},{4,5},{5,4},{6,7},{7,6},{8,9},{9,8},{10,11... | collective-permute-start | bytes 1179656 | tf_op jit(solution)/shard_map/ppermute | solution.py:248
  8.8 2.1 %prefilter.1 = (bf16[384,512]{1,0:T(8,128)(2,1)S(1)}, bf16[384,512]{1,0:T(8,128)(2,1)S(1)}, bf16[8,5632]{1,0:T(8,128)(2,1)S(1)}, f32[12,512]{1,0:T(8,128)S(1)}, ...) custom-call(bf16[8,24576]{1,0:T(8,128)(2,1)} %volt_hbm.1, f32[12,512]{1,0:T(8,128)} %taps_hbm.1, ...), custom_call_target="tpu_custom_call" | custom-call | flops 100000000 | bytes 4000000 | tf_op jit(solution)/shard_map/prefilter/pallas_call | solution.py:251
  10.9 0.0 collective-permute-done.other_ref
  10.9 1.4 %channelize.1 = bf16[2048,128]{1,0:T(8,128)(2,1)S(1)} custom-call(bf16[384,512]{1,0:T(8,128)(2,1)S(1)} %get-tuple-element.11.fhigh, bf16[384,512]{1,0:T(8,128)(2,1)S(1)} %get-tuple-element.12.flow, bf16[8,5632]{1,0:T(8,128)(2,1)S(1)} %get-tuple-element.13.seam, bf16[8,24576]{1,0:T(8,128)(2,1)S(1)} %collective-permute-done.other_ref, ...), custom_call_target="tpu_custom_call" | custom-call | tf_op jit(solution)/shard_map/channelize/pallas_call | solution.py:273
  12.3 36.3 %all_to_all.5 = bf16[256,8,128]{2,1,0:T(8,128)(2,1)S(1)} all-to-all(bf16[256,8,128]{2,1,0:T(8,128)(2,1)S(1)} %bitcast.4), channel_id=1, replica_groups=mesh['z'=8,'x'=4,'ylo'=4,'yhi'=2,'core'=2] {'yhi','z','x','ylo'}, dimensions={0} | all-to-all | bytes 1048576 | tf_op jit(solution)/shard_map/all_to_all | solution.py:287
  48.6 3.9 %collective-permute-start.1 = (bf16[2048,128]{1,0:T(8,128)(2,1)S(1)}, bf16[2048,128]{1,0:T(8,128)(2,1)S(1)}, u32[]{:S(2)}, u32[]{:S(2)}) collective-permute-start(bf16[2048,128]{1,0:T(8,128)(2,1)S(1)} %bitcast.2), channel_id=1, source_target_pairs={{0,1},{1,0},{2,3},{3,2},{4,5},{5,4},{6,7},{7,6},{8,9},{9,8},{10,11... | collective-permute-start | bytes 1572872 | tf_op jit(solution)/shard_map/ppermute | solution.py:291
  52.5 0.8 %first_half.1.refs_1_ = f32[4,2,256,256]{3,2,1,0:T(8,128)S(1)} custom-call(bf16[2048,128]{1,0:T(8,128)(2,1)S(1)} %bitcast.3), custom_call_target="tpu_custom_call" | custom-call | flops 300000000 | bytes 3000000 | tf_op jit(solution)/shard_map/first_half/pallas_call | solution.py:299
  53.3 0.8 %collective-permute-done.1.refs_0_ = bf16[2048,128]{1,0:T(8,128)(2,1)S(1)} collective-permute-done((bf16[2048,128]{1,0:T(8,128)(2,1)S(1)}, bf16[2048,128]{1,0:T(8,128)(2,1)S(1)}, u32[]{:S(2)}, u32[]{:S(2)}) %collective-permute-start.1) | collective-permute-done | bytes 524320 | tf_op jit(solution)/shard_map/ppermute | solution.py:291
  54.0 1.7 %second_half.1 = f32[2,1,256,1024]{3,2,1,0:T(8,128)} custom-call(bf16[2048,128]{1,0:T(8,128)(2,1)S(1)} %collective-permute-done.1.refs_0_, f32[4,2,256,256]{3,2,1,0:T(8,128)S(1)} %first_half.1.refs_1_), custom_call_target="tpu_custom_call" | custom-call | tf_op jit(solution)/shard_map/second_half/pallas_call | solution.py:310
Async XLA Ops:
  0.0 10.9 %collective-permute-start = (bf16[8,24576]{1,0:T(8,128)(2,1)}, bf16[8,24576]{1,0:T(8,128)(2,1)S(1)}, u32[]{:S(2)}, u32[]{:S(2)}) collective-permute-start(bf16[8,24576]{1,0:T(8,128)(2,1)} %volt_hbm.1), channel_id=1, source_target_pairs={{0,1},{1,0},{2,3},{3,2},{4,5},{5,4},{6,7},{7,6},{8,9},{9,8},{10,11... | collective-permute-start | bytes 1179656 | tf_op jit(solution)/shard_map/ppermute | solution.py:248
  48.6 5.4 %collective-permute-start.1 = (bf16[2048,128]{1,0:T(8,128)(2,1)S(1)}, bf16[2048,128]{1,0:T(8,128)(2,1)S(1)}, u32[]{:S(2)}, u32[]{:S(2)}) collective-permute-start(bf16[2048,128]{1,0:T(8,128)(2,1)S(1)} %bitcast.2), channel_id=1, source_target_pairs={{0,1},{1,0},{2,3},{3,2},{4,5},{5,4},{6,7},{7,6},{8,9},{9,8},{10,11... | collective-permute-start | bytes 1572872 | tf_op jit(solution)/shard_map/ppermute | solution.py:291

commit v5 on v4

--- a/solution.py
+++ b/solution.py
@@ -17,6 +17,7 @@
 N_IN = 8
 N_FR = 48
 N_TB = 4
+N_Y = 4
 SLOTS = N_FR + MARGIN
 HALF = 64
 LANES = 128
@@ -31,7 +32,8 @@
 
 
 def dft_tables():
-    phase = (np.arange(CH)[:, None] + OFFSET) * np.arange(FRAME)[None, :] % FRAME
+    channel = np.arange(CH).reshape(CH // N_Y, N_Y).T.reshape(-1)
+    phase = (channel[:, None] + OFFSET) * np.arange(FRAME)[None, :] % FRAME
     angle = phase * (2.0 * math.pi / FRAME)
     table = np.concatenate([np.cos(angle), -np.sin(angle)], 0) / math.sqrt(FRAME)
     high = table.astype(jnp.bfloat16)
@@ -185,6 +187,11 @@
         out_ref[copy * CH * N_IN : (copy + 1) * CH * N_IN, :] = result
 
 
+def natural(block):
+    by_y = block.reshape(N_Y, CH // N_Y, N_IN, LANES)
+    return jnp.stack([by_y[y] for y in range(N_Y)], axis=1).reshape(N_INPUTS, LANES)
+
+
 def lay(in_ref, cols_ref, rows_ref, parts):
     core, yhi = lax.axis_index("core"), lax.axis_index("yhi")
     rows = rows_ref.shape[1]
@@ -192,7 +199,8 @@
     @pl.when(jnp.logical_not(parts))
     def _():
         for t in range(2):
-            cols_ref[:, t * LANES : (t + 1) * LANES] = in_ref[t * N_INPUTS : (t + 1) * N_INPUTS, :]
+            block = natural(in_ref[t * N_INPUTS : (t + 1) * N_INPUTS, :].astype(jnp.float32))
+            cols_ref[:, t * LANES : (t + 1) * LANES] = block.astype(jnp.bfloat16)
 
     @pl.when(parts)
     def _():
@@ -204,8 +212,8 @@
         total = (a + pltpu.roll(a, MARGIN, 1)) + (b + pltpu.roll(b, MARGIN, 1))
         one = jnp.where(edge, total, jnp.where(low, 0.0, a))
         two = jnp.where(edge | low, 0.0, b)
-        cols_ref[:, :LANES] = one.astype(jnp.bfloat16)
-        cols_ref[:, LANES:] = two.astype(jnp.bfloat16)
+        cols_ref[:, :LANES] = natural(one).astype(jnp.bfloat16)
+        cols_ref[:, LANES:] = natural(two).astype(jnp.bfloat16)
 
     own = pl.multiple_of((yhi * 2 + core) * rows, rows)
     lanes = lane_ids(rows)
@@ -285,7 +293,7 @@
         name="channelize",
     )(fhigh, flow, seam, other, taps, high, low)
     turned = lax.all_to_all(
-        spectra.reshape(2 * CH, N_IN, LANES), ("yhi", "z", "x", "ylo"), 0, 0, tiled=True
+        spectra.reshape(2 * CH, N_IN, LANES), ("yhi", "ylo", "z", "x"), 0, 0, tiled=True
     )
     own = turned.reshape(2 * N_INPUTS, LANES)
     other_core = lax.ppermute(own, "core", SWAP)

time: 55.9 us -> 54.4 us (0.973)
  blocking collectives: 36.3 us -> 34.5 us
    all_to_all x1, blocking collectives: 36.3 us -> 34.5 us  [per_device(): lax.all_to_all(spectra.reshape(2 * CH, N_IN, LANES), ('yhi', 'ylo', 'z',...]
where the time goes in v5:
time: 54.4 us; the launch traced here: 54.2 us
  blocking collectives  34.5 us (63%)
  starting transfers between devices  12.9 us (24%)
  Pallas kernels  5.99 us (11%)
  waiting for transfers between devices  0.75 us (1%)
    all_to_all x1, blocking collectives, per_device(): lax.all_to_all(spectra.reshape(2 * CH, N_IN, LANES), ('yhi', 'ylo', 'z',...  34.5 us
    ppermute x1, starting transfers between devices, per_device(): other = lax.ppermute(voltages, 'core', SWAP)  8.77 us
    ppermute x1, starting transfers between devices, per_device(): other_core = lax.ppermute(own, 'core', SWAP)  4.16 us
    pallas_call x1, Pallas kernels, per_device(): pl.pallas_call(prefilter_kernel, out_shape=[jax.ShapeDtypeStruct((N_IN *...  2.11 us
    pallas_call x1, Pallas kernels, per_device(): pl.pallas_call(lambda *refs: second_half_kernel(scale, *refs), out_shape=...  1.72 us
    pallas_call x1, Pallas kernels, per_device(): pl.pallas_call(channelize_kernel, out_shape=jax.ShapeDtypeStruct((2 * CH...  1.38 us
  transfers between devices with their start and end apart: 2, of which 1 were waited for; matrix products, arithmetic and copies ran while one was open for 0% of the time, Pallas kernels for 5%

profile of v5, /device:TPU:1, one launch (start us, length us, event | category | flops | bytes accessed | tf_op | source)
XLA Modules:
  0.0 54.2 jit_solution(16528034324965607330)
XLA Ops:
  0.0 8.8 %collective-permute-start = (bf16[8,24576]{1,0:T(8,128)(2,1)}, bf16[8,24576]{1,0:T(8,128)(2,1)S(1)}, u32[]{:S(2)}, u32[]{:S(2)}) collective-permute-start(bf16[8,24576]{1,0:T(8,128)(2,1)} %volt_hbm.1), channel_id=1, source_target_pairs={{0,1},{1,0},{2,3},{3,2},{4,5},{5,4},{6,7},{7,6},{8,9},{9,8},{10,11... | collective-permute-start | bytes 1179656 | tf_op jit(solution)/shard_map/ppermute | solution.py:256
  8.8 2.1 %prefilter.1 = (bf16[384,512]{1,0:T(8,128)(2,1)S(1)}, bf16[384,512]{1,0:T(8,128)(2,1)S(1)}, bf16[8,5632]{1,0:T(8,128)(2,1)S(1)}, f32[12,512]{1,0:T(8,128)S(1)}, ...) custom-call(bf16[8,24576]{1,0:T(8,128)(2,1)} %volt_hbm.1, f32[12,512]{1,0:T(8,128)} %taps_hbm.1, ...), custom_call_target="tpu_custom_call" | custom-call | flops 100000000 | bytes 4000000 | tf_op jit(solution)/shard_map/prefilter/pallas_call | solution.py:259
  10.9 0.0 collective-permute-done.other_ref
  10.9 1.4 %channelize.1 = bf16[2048,128]{1,0:T(8,128)(2,1)S(1)} custom-call(bf16[384,512]{1,0:T(8,128)(2,1)S(1)} %get-tuple-element.11.fhigh, bf16[384,512]{1,0:T(8,128)(2,1)S(1)} %get-tuple-element.12.flow, bf16[8,5632]{1,0:T(8,128)(2,1)S(1)} %get-tuple-element.13.seam, bf16[8,24576]{1,0:T(8,128)(2,1)S(1)} %collective-permute-done.other_ref, ...), custom_call_target="tpu_custom_call" | custom-call | tf_op jit(solution)/shard_map/channelize/pallas_call | solution.py:281
  12.3 34.5 %all_to_all.5 = bf16[256,8,128]{2,1,0:T(8,128)(2,1)S(1)} all-to-all(bf16[256,8,128]{2,1,0:T(8,128)(2,1)S(1)} %bitcast.4), channel_id=1, replica_groups=mesh['z'=8,'x'=4,'ylo'=4,'yhi'=2,'core'=2] {'yhi','ylo','z','x'}, dimensions={0} | all-to-all | bytes 1048576 | tf_op jit(solution)/shard_map/all_to_all | solution.py:295
  46.8 4.2 %collective-permute-start.1 = (bf16[2048,128]{1,0:T(8,128)(2,1)S(1)}, bf16[2048,128]{1,0:T(8,128)(2,1)S(1)}, u32[]{:S(2)}, u32[]{:S(2)}) collective-permute-start(bf16[2048,128]{1,0:T(8,128)(2,1)S(1)} %bitcast.2), channel_id=1, source_target_pairs={{0,1},{1,0},{2,3},{3,2},{4,5},{5,4},{6,7},{7,6},{8,9},{9,8},{10,11... | collective-permute-start | bytes 1572872 | tf_op jit(solution)/shard_map/ppermute | solution.py:299
  51.0 0.8 %first_half.1.refs_1_ = f32[4,2,256,256]{3,2,1,0:T(8,128)S(1)} custom-call(bf16[2048,128]{1,0:T(8,128)(2,1)S(1)} %bitcast.3), custom_call_target="tpu_custom_call" | custom-call | flops 300000000 | bytes 3000000 | tf_op jit(solution)/shard_map/first_half/pallas_call | solution.py:307
  51.8 0.7 %collective-permute-done.1.refs_0_ = bf16[2048,128]{1,0:T(8,128)(2,1)S(1)} collective-permute-done((bf16[2048,128]{1,0:T(8,128)(2,1)S(1)}, bf16[2048,128]{1,0:T(8,128)(2,1)S(1)}, u32[]{:S(2)}, u32[]{:S(2)}) %collective-permute-start.1) | collective-permute-done | bytes 524320 | tf_op jit(solution)/shard_map/ppermute | solution.py:299
  52.5 1.7 %second_half.1 = f32[2,1,256,1024]{3,2,1,0:T(8,128)} custom-call(bf16[2048,128]{1,0:T(8,128)(2,1)S(1)} %collective-permute-done.1.refs_0_, f32[4,2,256,256]{3,2,1,0:T(8,128)S(1)} %first_half.1.refs_1_), custom_call_target="tpu_custom_call" | custom-call | tf_op jit(solution)/shard_map/second_half/pallas_call | solution.py:318
Async XLA Ops:
  0.0 10.9 %collective-permute-start = (bf16[8,24576]{1,0:T(8,128)(2,1)}, bf16[8,24576]{1,0:T(8,128)(2,1)S(1)}, u32[]{:S(2)}, u32[]{:S(2)}) collective-permute-start(bf16[8,24576]{1,0:T(8,128)(2,1)} %volt_hbm.1), channel_id=1, source_target_pairs={{0,1},{1,0},{2,3},{3,2},{4,5},{5,4},{6,7},{7,6},{8,9},{9,8},{10,11... | collective-permute-start | bytes 1179656 | tf_op jit(solution)/shard_map/ppermute | solution.py:256
  46.8 5.7 %collective-permute-start.1 = (bf16[2048,128]{1,0:T(8,128)(2,1)S(1)}, bf16[2048,128]{1,0:T(8,128)(2,1)S(1)}, u32[]{:S(2)}, u32[]{:S(2)}) collective-permute-start(bf16[2048,128]{1,0:T(8,128)(2,1)S(1)} %bitcast.2), channel_id=1, source_target_pairs={{0,1},{1,0},{2,3},{3,2},{4,5},{5,4},{6,7},{7,6},{8,9},{9,8},{10,11... | collective-permute-start | bytes 1572872 | tf_op jit(solution)/shard_map/ppermute | solution.py:299

commit v6 on v4

--- a/solution.py
+++ b/solution.py
@@ -17,6 +17,8 @@
 N_IN = 8
 N_FR = 48
 N_TB = 4
+SIZES = (8, 4, 4, 2, 2)
+AXES = ("z", "x", "ylo", "yhi", "core")
 SLOTS = N_FR + MARGIN
 HALF = 64
 LANES = 128
@@ -28,6 +30,23 @@
 
 LOW_SLOT = N_FR - MARGIN
 HIGH_SLOT = N_FR
+SEED = 1
+
+
+def listing():
+    y, z, x = np.meshgrid(np.arange(8), np.arange(8), np.arange(4), indexing="ij")
+    owners = np.stack([y // 4, (z * 4 + x) * 4 + y % 4], -1).reshape(-1, 2)
+    return owners[np.random.RandomState(SEED).permutation(2 * CH)]
+
+
+OWNERS = listing()
+PLACE = np.zeros((2, CH), np.int64)
+PLACE[OWNERS[:, 0], OWNERS[:, 1]] = np.arange(2 * CH)
+
+
+def groups():
+    yhi, station = OWNERS[:, 0], OWNERS[:, 1]
+    return [[int(p) for p in (station * 2 + yhi) * 2 + core] for core in range(2)]
 
 
 def dft_tables():
@@ -180,32 +199,44 @@
             value = jnp.where(split, pltpu.roll(rest, LANES - MARGIN, 1), value)
             value = jnp.where(drop, 0.0, value)
             spread[pl.ds(i + sub, CH, stride=N_IN), :] = value
-    result = spread[...].astype(jnp.bfloat16)
-    for copy in range(2):
-        out_ref[copy * CH * N_IN : (copy + 1) * CH * N_IN, :] = result
+    for pair in range(CH):
+        two = [spread[int(c) * N_IN : (int(c) + 1) * N_IN, :] for c in OWNERS[2 * pair : 2 * pair + 2, 1]]
+        out_ref[pair * 2 * N_IN : (pair + 1) * 2 * N_IN, :] = jnp.concatenate(two, 0).astype(jnp.bfloat16)
+
+
+def two_tiles(in_ref, yhi, pair):
+    tiles = []
+    for place in PLACE[yhi, 2 * pair : 2 * pair + 2]:
+        both = in_ref[int(place) // 2 * 2 * N_IN : (int(place) // 2 + 1) * 2 * N_IN, :].astype(jnp.float32)
+        tiles.append(both[int(place) % 2 * N_IN : (int(place) % 2 + 1) * N_IN])
+    return jnp.concatenate(tiles, 0)
 
 
 def lay(in_ref, cols_ref, rows_ref, parts):
     core, yhi = lax.axis_index("core"), lax.axis_index("yhi")
     rows = rows_ref.shape[1]
+    step = 2 * N_IN
 
     @pl.when(jnp.logical_not(parts))
     def _():
-        for t in range(2):
-            cols_ref[:, t * LANES : (t + 1) * LANES] = in_ref[t * N_INPUTS : (t + 1) * N_INPUTS, :]
+        for pair in range(CH // 2):
+            for t in range(2):
+                value = two_tiles(in_ref, t, pair).astype(jnp.bfloat16)
+                cols_ref[pair * step : (pair + 1) * step, t * LANES : (t + 1) * LANES] = value
 
     @pl.when(parts)
     def _():
-        slot = lane_ids(N_INPUTS) % HALF
+        slot = lane_ids(step) % HALF
         edge = (slot >= HIGH_SLOT) & (slot < SLOTS)
         low = (slot >= LOW_SLOT) & (slot < HIGH_SLOT)
-        a = in_ref[:N_INPUTS, :].astype(jnp.float32)
-        b = in_ref[N_INPUTS:, :].astype(jnp.float32)
-        total = (a + pltpu.roll(a, MARGIN, 1)) + (b + pltpu.roll(b, MARGIN, 1))
-        one = jnp.where(edge, total, jnp.where(low, 0.0, a))
-        two = jnp.where(edge | low, 0.0, b)
-        cols_ref[:, :LANES] = one.astype(jnp.bfloat16)
-        cols_ref[:, LANES:] = two.astype(jnp.bfloat16)
+        for pair in range(CH // 2):
+            a, b = two_tiles(in_ref, 0, pair), two_tiles(in_ref, 1, pair)
+            total = (a + pltpu.roll(a, MARGIN, 1)) + (b + pltpu.roll(b, MARGIN, 1))
+            one = jnp.where(edge, total, jnp.where(low, 0.0, a))
+            two = jnp.where(edge | low, 0.0, b)
+            cut = slice(pair * step, (pair + 1) * step)
+            cols_ref[cut, :LANES] = one.astype(jnp.bfloat16)
+            cols_ref[cut, LANES:] = two.astype(jnp.bfloat16)
 
     own = pl.multiple_of((yhi * 2 + core) * rows, rows)
     lanes = lane_ids(rows)
@@ -285,7 +316,7 @@
         name="channelize",
     )(fhigh, flow, seam, other, taps, high, low)
     turned = lax.all_to_all(
-        spectra.reshape(2 * CH, N_IN, LANES), ("yhi", "z", "x", "ylo"), 0, 0, tiled=True
+        spectra.reshape(2 * CH, N_IN, LANES), AXES, 0, 0, axis_index_groups=groups(), tiled=True
     )
     own = turned.reshape(2 * N_INPUTS, LANES)
     other_core = lax.ppermute(own, "core", SWAP)
@@ -323,7 +354,7 @@
 
 
 def solution(mesh):
-    fine = Mesh(mesh.devices.reshape(8, 4, 4, 2, 2), ("z", "x", "ylo", "yhi", "core"))
+    fine = Mesh(mesh.devices.reshape(SIZES), AXES)
     in_specs = (P(("z", "x", "ylo"), ("yhi", "core")), P())
     out_specs = P(None, ("z", "x", "ylo"), ("yhi", "core"), None)
     return jax.shard_map(

time: 55.9 us -> 49.3 us (0.88)
  blocking collectives: 36.3 us -> 31 us
  starting transfers between devices: 12.7 us -> 11.4 us
    all_to_all x1, blocking collectives: 36.3 us -> 31 us  [per_device(): lax.all_to_all(spectra.reshape(2 * CH, N_IN, LANES), AXES, 0, 0, axis_ind...]
    ppermute x1, starting transfers between devices: 3.88 us -> 2.6 us  [per_device(): other_core = lax.ppermute(own, 'core', SWAP)]
  transfers between devices with their start and end apart: 2 -> 2, of which waited for: 1 -> 1; matrix products, arithmetic and copies ran while one was open for 0% -> 0% of each run, Pallas kernels for 5% -> 6%
where the time goes in v6:
time: 49.3 us; the launch traced here: 49.1 us
  blocking collectives  31 us (63%)
  starting transfers between devices  11.4 us (23%)
  Pallas kernels  5.94 us (12%)
  waiting for transfers between devices  0.81 us (2%)
    all_to_all x1, blocking collectives, per_device(): lax.all_to_all(spectra.reshape(2 * CH, N_IN, LANES), AXES, 0, 0, axis_ind...  31 us
    ppermute x1, starting transfers between devices, per_device(): other = lax.ppermute(voltages, 'core', SWAP)  8.77 us
    ppermute x1, starting transfers between devices, per_device(): other_core = lax.ppermute(own, 'core', SWAP)  2.6 us
    pallas_call x1, Pallas kernels, per_device(): pl.pallas_call(prefilter_kernel, out_shape=[jax.ShapeDtypeStruct((N_IN *...  2.11 us
    pallas_call x1, Pallas kernels, per_device(): pl.pallas_call(lambda *refs: second_half_kernel(scale, *refs), out_shape=...  1.72 us
    pallas_call x1, Pallas kernels, per_device(): pl.pallas_call(channelize_kernel, out_shape=jax.ShapeDtypeStruct((2 * CH...  1.4 us
  transfers between devices with their start and end apart: 2, of which 1 were waited for; matrix products, arithmetic and copies ran while one was open for 0% of the time, Pallas kernels for 6%

profile of v6, /device:TPU:1, one launch (start us, length us, event | category | flops | bytes accessed | tf_op | source)
XLA Modules:
  0.0 49.1 jit_solution(12626580988776152776)
XLA Ops:
  0.0 8.8 %collective-permute-start = (bf16[8,24576]{1,0:T(8,128)(2,1)}, bf16[8,24576]{1,0:T(8,128)(2,1)S(1)}, u32[]{:S(2)}, u32[]{:S(2)}) collective-permute-start(bf16[8,24576]{1,0:T(8,128)(2,1)} %volt_hbm.1), channel_id=1, source_target_pairs={{0,1},{1,0},{2,3},{3,2},{4,5},{5,4},{6,7},{7,6},{8,9},{9,8},{10,11... | collective-permute-start | bytes 1179656 | tf_op jit(solution)/shard_map/ppermute | solution.py:279
  8.8 2.1 %prefilter.1 = (bf16[384,512]{1,0:T(8,128)(2,1)S(1)}, bf16[384,512]{1,0:T(8,128)(2,1)S(1)}, bf16[8,5632]{1,0:T(8,128)(2,1)S(1)}, f32[12,512]{1,0:T(8,128)S(1)}, ...) custom-call(bf16[8,24576]{1,0:T(8,128)(2,1)} %volt_hbm.1, f32[12,512]{1,0:T(8,128)} %taps_hbm.1, ...), custom_call_target="tpu_custom_call" | custom-call | flops 100000000 | bytes 4000000 | tf_op jit(solution)/shard_map/prefilter/pallas_call | solution.py:282
  10.9 0.0 collective-permute-done.other_ref
  10.9 1.4 %channelize.1 = bf16[2048,128]{1,0:T(8,128)(2,1)S(1)} custom-call(bf16[384,512]{1,0:T(8,128)(2,1)S(1)} %get-tuple-element.11.fhigh, bf16[384,512]{1,0:T(8,128)(2,1)S(1)} %get-tuple-element.12.flow, bf16[8,5632]{1,0:T(8,128)(2,1)S(1)} %get-tuple-element.13.seam, bf16[8,24576]{1,0:T(8,128)(2,1)S(1)} %collective-permute-done.other_ref, ...), custom_call_target="tpu_custom_call" | custom-call | tf_op jit(solution)/shard_map/channelize/pallas_call | solution.py:304
  12.3 31.0 %all_to_all.5 = bf16[256,8,128]{2,1,0:T(8,128)(2,1)S(1)} all-to-all(bf16[256,8,128]{2,1,0:T(8,128)(2,1)S(1)} %bitcast.4), channel_id=1, replica_groups={{374,36,406,158,394,342,6,432,274,438,510,484,64,94,196,54,414,308,358,..., dimensions={0} | all-to-all | bytes 1048576 | tf_op jit(solution)/shard_map/all_to_all | solution.py:318
  43.3 2.6 %collective-permute-start.1 = (bf16[2048,128]{1,0:T(8,128)(2,1)S(1)}, bf16[2048,128]{1,0:T(8,128)(2,1)S(1)}, u32[]{:S(2)}, u32[]{:S(2)}) collective-permute-start(bf16[2048,128]{1,0:T(8,128)(2,1)S(1)} %bitcast.2), channel_id=1, source_target_pairs={{0,1},{1,0},{2,3},{3,2},{4,5},{5,4},{6,7},{7,6},{8,9},{9,8},{10,11... | collective-permute-start | bytes 1572872 | tf_op jit(solution)/shard_map/ppermute | solution.py:322
  45.9 0.7 %first_half.1.refs_1_ = f32[4,2,256,256]{3,2,1,0:T(8,128)S(1)} custom-call(bf16[2048,128]{1,0:T(8,128)(2,1)S(1)} %bitcast.3), custom_call_target="tpu_custom_call" | custom-call | flops 300000000 | bytes 3000000 | tf_op jit(solution)/shard_map/first_half/pallas_call | solution.py:330
  46.6 0.8 %collective-permute-done.1.refs_0_ = bf16[2048,128]{1,0:T(8,128)(2,1)S(1)} collective-permute-done((bf16[2048,128]{1,0:T(8,128)(2,1)S(1)}, bf16[2048,128]{1,0:T(8,128)(2,1)S(1)}, u32[]{:S(2)}, u32[]{:S(2)}) %collective-permute-start.1) | collective-permute-done | bytes 524320 | tf_op jit(solution)/shard_map/ppermute | solution.py:322
  47.4 1.7 %second_half.1 = f32[2,1,256,1024]{3,2,1,0:T(8,128)} custom-call(bf16[2048,128]{1,0:T(8,128)(2,1)S(1)} %collective-permute-done.1.refs_0_, f32[4,2,256,256]{3,2,1,0:T(8,128)S(1)} %first_half.1.refs_1_), custom_call_target="tpu_custom_call" | custom-call | tf_op jit(solution)/shard_map/second_half/pallas_call | solution.py:341
Async XLA Ops:
  0.0 10.9 %collective-permute-start = (bf16[8,24576]{1,0:T(8,128)(2,1)}, bf16[8,24576]{1,0:T(8,128)(2,1)S(1)}, u32[]{:S(2)}, u32[]{:S(2)}) collective-permute-start(bf16[8,24576]{1,0:T(8,128)(2,1)} %volt_hbm.1), channel_id=1, source_target_pairs={{0,1},{1,0},{2,3},{3,2},{4,5},{5,4},{6,7},{7,6},{8,9},{9,8},{10,11... | collective-permute-start | bytes 1179656 | tf_op jit(solution)/shard_map/ppermute | solution.py:279
  43.3 4.1 %collective-permute-start.1 = (bf16[2048,128]{1,0:T(8,128)(2,1)S(1)}, bf16[2048,128]{1,0:T(8,128)(2,1)S(1)}, u32[]{:S(2)}, u32[]{:S(2)}) collective-permute-start(bf16[2048,128]{1,0:T(8,128)(2,1)S(1)} %bitcast.2), channel_id=1, source_target_pairs={{0,1},{1,0},{2,3},{3,2},{4,5},{5,4},{6,7},{7,6},{8,9},{9,8},{10,11... | collective-permute-start | bytes 1572872 | tf_op jit(solution)/shard_map/ppermute | solution.py:322

commit v7 on v6

--- a/solution.py
+++ b/solution.py
@@ -30,7 +30,7 @@
 
 LOW_SLOT = N_FR - MARGIN
 HIGH_SLOT = N_FR
-SEED = 1
+SEED = 8
 
 
 def listing():
@@ -74,7 +74,7 @@
 
 
 def run_filter(taps_ref, frame_at, keep, count, block):
-    lo = pl.multiple_of(block * LANES, LANES)
+    lo = block * LANES if isinstance(block, int) else pl.multiple_of(block * LANES, LANES)
     taps = [jnp.broadcast_to(taps_ref[k : k + 1, pl.ds(lo, LANES)], (N_IN, LANES)) for k in range(TAPS)]
     window = []
     for t in range(count + MARGIN):
@@ -94,6 +94,8 @@
 
 
 def at(t, lo):
+    if isinstance(lo, int):
+        return slice(t * FRAME + lo, t * FRAME + lo + LANES)
     return pl.ds(pl.multiple_of(t * FRAME + lo, LANES), LANES)
 
 
@@ -138,9 +140,8 @@
 
     seam[...] = frames[:, own:]
 
-    @pl.loop(0, FRAME // LANES)
-    def _(block):
-        def keep(f, x):
+    for block in range(FRAME // LANES):
+        def keep(f, x, block=block):
             filt[block, f * N_IN : (f + 1) * N_IN, :] = x
 
         run_filter(taps_ref, lambda t, lo: frames[:, at(t, lo)], keep, N_FR, block)
@@ -164,9 +165,8 @@
             return seam[:, at(t, lo)]
         return jnp.where(real_samples, other_ref[:, at(t - MARGIN, lo)].astype(jnp.float32), 0.0)
 
-    @pl.loop(0, FRAME // LANES)
-    def _(block):
-        def keep(f, x):
+    for block in range(FRAME // LANES):
+        def keep(f, x, block=block):
             filt[block, f * N_IN : (f + 1) * N_IN, :] = x
 
         run_filter(taps_ref, frame_at, keep, MARGIN, block)

time: 49.3 us -> 49 us (level)
  blocking collectives: 31 us -> 30.4 us
    all_to_all x1, blocking collectives: 31 us -> 30.4 us  [per_device(): lax.all_to_all(spectra.reshape(2 * CH, N_IN, LANES), AXES, 0, 0, axis_ind...]
where the time goes in v7:
time: 49 us; the launch traced here: 48.7 us
  blocking collectives  30.4 us (62%)
  starting transfers between devices  11.7 us (24%)
  Pallas kernels  5.78 us (12%)
  waiting for transfers between devices  0.81 us (2%)
    all_to_all x1, blocking collectives, per_device(): lax.all_to_all(spectra.reshape(2 * CH, N_IN, LANES), AXES, 0, 0, axis_ind...  30.4 us
    ppermute x1, starting transfers between devices, per_device(): other = lax.ppermute(voltages, 'core', SWAP)  8.77 us
    ppermute x1, starting transfers between devices, per_device(): other_core = lax.ppermute(own, 'core', SWAP)  2.91 us
    pallas_call x1, Pallas kernels, per_device(): pl.pallas_call(prefilter_kernel, out_shape=[jax.ShapeDtypeStruct((N_IN *...  2.06 us
    pallas_call x1, Pallas kernels, per_device(): pl.pallas_call(lambda *refs: second_half_kernel(scale, *refs), out_shape=...  1.72 us
    pallas_call x1, Pallas kernels, per_device(): pl.pallas_call(channelize_kernel, out_shape=jax.ShapeDtypeStruct((2 * CH...  1.28 us
  transfers between devices with their start and end apart: 2, of which 1 were waited for; matrix products, arithmetic and copies ran while one was open for 0% of the time, Pallas kernels for 6%

profile of v7, /device:TPU:1, one launch (start us, length us, event | category | flops | bytes accessed | tf_op | source)
XLA Modules:
  0.0 48.7 jit_solution(8330845197581470441)
XLA Ops:
  0.0 8.8 %collective-permute-start = (bf16[8,24576]{1,0:T(8,128)(2,1)}, bf16[8,24576]{1,0:T(8,128)(2,1)S(1)}, u32[]{:S(2)}, u32[]{:S(2)}) collective-permute-start(bf16[8,24576]{1,0:T(8,128)(2,1)} %volt_hbm.1), channel_id=1, source_target_pairs={{0,1},{1,0},{2,3},{3,2},{4,5},{5,4},{6,7},{7,6},{8,9},{9,8},{10,11... | collective-permute-start | bytes 1179656 | tf_op jit(solution)/shard_map/ppermute | solution.py:279
  8.8 2.1 %prefilter.1 = (bf16[384,512]{1,0:T(8,128)(2,1)S(1)}, bf16[384,512]{1,0:T(8,128)(2,1)S(1)}, bf16[8,5632]{1,0:T(8,128)(2,1)S(1)}, f32[12,512]{1,0:T(8,128)S(1)}, ...) custom-call(bf16[8,24576]{1,0:T(8,128)(2,1)} %volt_hbm.1, f32[12,512]{1,0:T(8,128)} %taps_hbm.1, ...), custom_call_target="tpu_custom_call" | custom-call | flops 100000000 | bytes 4000000 | tf_op jit(solution)/shard_map/prefilter/pallas_call | solution.py:282
  10.9 0.0 collective-permute-done.other_ref
  10.9 1.3 %channelize.1 = bf16[2048,128]{1,0:T(8,128)(2,1)S(1)} custom-call(bf16[384,512]{1,0:T(8,128)(2,1)S(1)} %get-tuple-element.11.fhigh, bf16[384,512]{1,0:T(8,128)(2,1)S(1)} %get-tuple-element.12.flow, bf16[8,5632]{1,0:T(8,128)(2,1)S(1)} %get-tuple-element.13.seam, bf16[8,24576]{1,0:T(8,128)(2,1)S(1)} %collective-permute-done.other_ref, ...), custom_call_target="tpu_custom_call" | custom-call | tf_op jit(solution)/shard_map/channelize/pallas_call | solution.py:304
  12.2 30.4 %all_to_all.5 = bf16[256,8,128]{2,1,0:T(8,128)(2,1)S(1)} all-to-all(bf16[256,8,128]{2,1,0:T(8,128)(2,1)S(1)} %bitcast.4), channel_id=1, replica_groups={{354,334,264,326,406,400,222,480,232,136,48,470,456,36,202,270,252,172,..., dimensions={0} | all-to-all | bytes 1048576 | tf_op jit(solution)/shard_map/all_to_all | solution.py:318
  42.6 2.9 %collective-permute-start.1 = (bf16[2048,128]{1,0:T(8,128)(2,1)S(1)}, bf16[2048,128]{1,0:T(8,128)(2,1)S(1)}, u32[]{:S(2)}, u32[]{:S(2)}) collective-permute-start(bf16[2048,128]{1,0:T(8,128)(2,1)S(1)} %bitcast.2), channel_id=1, source_target_pairs={{0,1},{1,0},{2,3},{3,2},{4,5},{5,4},{6,7},{7,6},{8,9},{9,8},{10,11... | collective-permute-start | bytes 1572872 | tf_op jit(solution)/shard_map/ppermute | solution.py:322
  45.5 0.7 %first_half.1.refs_1_ = f32[4,2,256,256]{3,2,1,0:T(8,128)S(1)} custom-call(bf16[2048,128]{1,0:T(8,128)(2,1)S(1)} %bitcast.3), custom_call_target="tpu_custom_call" | custom-call | flops 300000000 | bytes 3000000 | tf_op jit(solution)/shard_map/first_half/pallas_call | solution.py:330
  46.2 0.8 %collective-permute-done.1.refs_0_ = bf16[2048,128]{1,0:T(8,128)(2,1)S(1)} collective-permute-done((bf16[2048,128]{1,0:T(8,128)(2,1)S(1)}, bf16[2048,128]{1,0:T(8,128)(2,1)S(1)}, u32[]{:S(2)}, u32[]{:S(2)}) %collective-permute-start.1) | collective-permute-done | bytes 524320 | tf_op jit(solution)/shard_map/ppermute | solution.py:322
  47.0 1.7 %second_half.1 = f32[2,1,256,1024]{3,2,1,0:T(8,128)} custom-call(bf16[2048,128]{1,0:T(8,128)(2,1)S(1)} %collective-permute-done.1.refs_0_, f32[4,2,256,256]{3,2,1,0:T(8,128)S(1)} %first_half.1.refs_1_), custom_call_target="tpu_custom_call" | custom-call | tf_op jit(solution)/shard_map/second_half/pallas_call | solution.py:341
Async XLA Ops:
  0.0 10.9 %collective-permute-start = (bf16[8,24576]{1,0:T(8,128)(2,1)}, bf16[8,24576]{1,0:T(8,128)(2,1)S(1)}, u32[]{:S(2)}, u32[]{:S(2)}) collective-permute-start(bf16[8,24576]{1,0:T(8,128)(2,1)} %volt_hbm.1), channel_id=1, source_target_pairs={{0,1},{1,0},{2,3},{3,2},{4,5},{5,4},{6,7},{7,6},{8,9},{9,8},{10,11... | collective-permute-start | bytes 1179656 | tf_op jit(solution)/shard_map/ppermute | solution.py:279
  42.6 4.4 %collective-permute-start.1 = (bf16[2048,128]{1,0:T(8,128)(2,1)S(1)}, bf16[2048,128]{1,0:T(8,128)(2,1)S(1)}, u32[]{:S(2)}, u32[]{:S(2)}) collective-permute-start(bf16[2048,128]{1,0:T(8,128)(2,1)S(1)} %bitcast.2), channel_id=1, source_target_pairs={{0,1},{1,0},{2,3},{3,2},{4,5},{5,4},{6,7},{7,6},{8,9},{9,8},{10,11... | collective-permute-start | bytes 1572872 | tf_op jit(solution)/shard_map/ppermute | solution.py:322

commit v8 on v7

--- a/solution.py
+++ b/solution.py
@@ -321,7 +321,7 @@
     own = turned.reshape(2 * N_INPUTS, LANES)
     other_core = lax.ppermute(own, "core", SWAP)
     rows = N_INPUTS // N_TB
-    cols = 256
+    cols = 512
     chunks = N_INPUTS // cols
     operands = [
         pltpu.VMEM((N_INPUTS, 2 * LANES), jnp.bfloat16),

time: 49 us -> 48.9 us (level)
  no operation moved by 1% of the time
where the time goes in v8:
time: 48.9 us; the launch traced here: 48.7 us
  blocking collectives  30.4 us (62%)
  starting transfers between devices  11.7 us (24%)
  Pallas kernels  5.76 us (12%)
  waiting for transfers between devices  0.81 us (2%)
    all_to_all x1, blocking collectives, per_device(): lax.all_to_all(spectra.reshape(2 * CH, N_IN, LANES), AXES, 0, 0, axis_ind...  30.4 us
    ppermute x1, starting transfers between devices, per_device(): other = lax.ppermute(voltages, 'core', SWAP)  8.77 us
    ppermute x1, starting transfers between devices, per_device(): other_core = lax.ppermute(own, 'core', SWAP)  2.91 us
    pallas_call x1, Pallas kernels, per_device(): pl.pallas_call(prefilter_kernel, out_shape=[jax.ShapeDtypeStruct((N_IN *...  2.06 us
    pallas_call x1, Pallas kernels, per_device(): pl.pallas_call(lambda *refs: second_half_kernel(scale, *refs), out_shape=...  1.71 us
    pallas_call x1, Pallas kernels, per_device(): pl.pallas_call(channelize_kernel, out_shape=jax.ShapeDtypeStruct((2 * CH...  1.28 us
  transfers between devices with their start and end apart: 2, of which 1 were waited for; matrix products, arithmetic and copies ran while one was open for 0% of the time, Pallas kernels for 6%

profile of v8, /device:TPU:1, one launch (start us, length us, event | category | flops | bytes accessed | tf_op | source)
XLA Modules:
  0.0 48.7 jit_solution(11585840021316197349)
XLA Ops:
  0.0 8.8 %collective-permute-start = (bf16[8,24576]{1,0:T(8,128)(2,1)}, bf16[8,24576]{1,0:T(8,128)(2,1)S(1)}, u32[]{:S(2)}, u32[]{:S(2)}) collective-permute-start(bf16[8,24576]{1,0:T(8,128)(2,1)} %volt_hbm.1), channel_id=1, source_target_pairs={{0,1},{1,0},{2,3},{3,2},{4,5},{5,4},{6,7},{7,6},{8,9},{9,8},{10,11... | collective-permute-start | bytes 1179656 | tf_op jit(solution)/shard_map/ppermute | solution.py:279
  8.8 2.1 %prefilter.1 = (bf16[384,512]{1,0:T(8,128)(2,1)S(1)}, bf16[384,512]{1,0:T(8,128)(2,1)S(1)}, bf16[8,5632]{1,0:T(8,128)(2,1)S(1)}, f32[12,512]{1,0:T(8,128)S(1)}, ...) custom-call(bf16[8,24576]{1,0:T(8,128)(2,1)} %volt_hbm.1, f32[12,512]{1,0:T(8,128)} %taps_hbm.1, ...), custom_call_target="tpu_custom_call" | custom-call | flops 100000000 | bytes 4000000 | tf_op jit(solution)/shard_map/prefilter/pallas_call | solution.py:282
  10.9 0.0 collective-permute-done.other_ref
  10.9 1.3 %channelize.1 = bf16[2048,128]{1,0:T(8,128)(2,1)S(1)} custom-call(bf16[384,512]{1,0:T(8,128)(2,1)S(1)} %get-tuple-element.11.fhigh, bf16[384,512]{1,0:T(8,128)(2,1)S(1)} %get-tuple-element.12.flow, bf16[8,5632]{1,0:T(8,128)(2,1)S(1)} %get-tuple-element.13.seam, bf16[8,24576]{1,0:T(8,128)(2,1)S(1)} %collective-permute-done.other_ref, ...), custom_call_target="tpu_custom_call" | custom-call | tf_op jit(solution)/shard_map/channelize/pallas_call | solution.py:304
  12.2 30.4 %all_to_all.5 = bf16[256,8,128]{2,1,0:T(8,128)(2,1)S(1)} all-to-all(bf16[256,8,128]{2,1,0:T(8,128)(2,1)S(1)} %bitcast.4), channel_id=1, replica_groups={{354,334,264,326,406,400,222,480,232,136,48,470,456,36,202,270,252,172,..., dimensions={0} | all-to-all | bytes 1048576 | tf_op jit(solution)/shard_map/all_to_all | solution.py:318
  42.6 2.9 %collective-permute-start.1 = (bf16[2048,128]{1,0:T(8,128)(2,1)S(1)}, bf16[2048,128]{1,0:T(8,128)(2,1)S(1)}, u32[]{:S(2)}, u32[]{:S(2)}) collective-permute-start(bf16[2048,128]{1,0:T(8,128)(2,1)S(1)} %bitcast.2), channel_id=1, source_target_pairs={{0,1},{1,0},{2,3},{3,2},{4,5},{5,4},{6,7},{7,6},{8,9},{9,8},{10,11... | collective-permute-start | bytes 1572872 | tf_op jit(solution)/shard_map/ppermute | solution.py:322
  45.5 0.7 %first_half.1.refs_1_ = f32[2,2,256,512]{3,2,1,0:T(8,128)S(1)} custom-call(bf16[2048,128]{1,0:T(8,128)(2,1)S(1)} %bitcast.3), custom_call_target="tpu_custom_call" | custom-call | flops 300000000 | bytes 3000000 | tf_op jit(solution)/shard_map/first_half/pallas_call | solution.py:330
  46.2 0.8 %collective-permute-done.1.refs_0_ = bf16[2048,128]{1,0:T(8,128)(2,1)S(1)} collective-permute-done((bf16[2048,128]{1,0:T(8,128)(2,1)S(1)}, bf16[2048,128]{1,0:T(8,128)(2,1)S(1)}, u32[]{:S(2)}, u32[]{:S(2)}) %collective-permute-start.1) | collective-permute-done | bytes 524320 | tf_op jit(solution)/shard_map/ppermute | solution.py:322
  47.0 1.7 %second_half.1 = f32[2,1,256,1024]{3,2,1,0:T(8,128)} custom-call(bf16[2048,128]{1,0:T(8,128)(2,1)S(1)} %collective-permute-done.1.refs_0_, f32[2,2,256,512]{3,2,1,0:T(8,128)S(1)} %first_half.1.refs_1_), custom_call_target="tpu_custom_call" | custom-call | tf_op jit(solution)/shard_map/second_half/pallas_call | solution.py:341
Async XLA Ops:
  0.0 10.9 %collective-permute-start = (bf16[8,24576]{1,0:T(8,128)(2,1)}, bf16[8,24576]{1,0:T(8,128)(2,1)S(1)}, u32[]{:S(2)}, u32[]{:S(2)}) collective-permute-start(bf16[8,24576]{1,0:T(8,128)(2,1)} %volt_hbm.1), channel_id=1, source_target_pairs={{0,1},{1,0},{2,3},{3,2},{4,5},{5,4},{6,7},{7,6},{8,9},{9,8},{10,11... | collective-permute-start | bytes 1179656 | tf_op jit(solution)/shard_map/ppermute | solution.py:279
  42.6 4.4 %collective-permute-start.1 = (bf16[2048,128]{1,0:T(8,128)(2,1)S(1)}, bf16[2048,128]{1,0:T(8,128)(2,1)S(1)}, u32[]{:S(2)}, u32[]{:S(2)}) collective-permute-start(bf16[2048,128]{1,0:T(8,128)(2,1)S(1)} %bitcast.2), channel_id=1, source_target_pairs={{0,1},{1,0},{2,3},{3,2},{4,5},{5,4},{6,7},{7,6},{8,9},{9,8},{10,11... | collective-permute-start | bytes 1572872 | tf_op jit(solution)/shard_map/ppermute | solution.py:322
